TPU v7x, 256 devices: a whole 4x4x8 slice. The times are simulated.
256 devices in a mesh: cuts: 4 (over y_hi, core), fsdp: 64 (over y_lo, z, x).
Axes of the slice: x: 4, y: 4 (y_hi: 2, y_lo: 2; y = y_hi * 2 + y_lo), z: 8, core: 2. Of those that a mesh axis runs over, the one named last changes fastest.
Arguments:
- hid_shared: bfloat16 [196608, 1536], P(('cuts', 'fsdp')), may hold values from -24 to 24
- hid_routed: bfloat16 [24576, 768], P(('cuts', 'fsdp')), may hold values from -96 to 96
- out_grad: bfloat16 [196608, 2560], P(('cuts', 'fsdp')), may hold values from -0.040527344 to 0.040527344
- slot_token: int32 [24576], P(('cuts', 'fsdp')), may hold values from 0 to 767, as said below
- slot_count: int32 [256], P(('cuts', 'fsdp')), may hold values from 24 to 96, as said below
- master_shared: float32 [1536, 2560], P(('cuts', 'fsdp')), may hold values from -6 to 6
- moment_shared: float32 [1536, 2560], P(('cuts', 'fsdp')), may hold values from -1.8 to 1.8
- second_shared: float32 [1536, 2560], P(('cuts', 'fsdp')), may hold values from 0.01 to 1
- master_routed: float32 [768, 2560], P(('cuts', 'fsdp')), may hold values from -6 to 6
- moment_routed: float32 [768, 2560], P(('cuts', 'fsdp')), may hold values from -1.8 to 1.8
- second_routed: float32 [768, 2560], P(('cuts', 'fsdp')), may hold values from 0.01 to 1
Outputs:
- new_moment_shared: float32 [1536, 2560], P(('cuts', 'fsdp'))
- new_second_shared: float32 [1536, 2560], P(('cuts', 'fsdp'))
- new_moment_routed: float32 [768, 2560], P(('cuts', 'fsdp'))
- new_second_routed: float32 [768, 2560], P(('cuts', 'fsdp'))
- weight_shared: bfloat16 [1536, 2560], P('cuts')
- weight_routed: bfloat16 [768, 2560], P('cuts')
Inputs may be any that keep to these rules, and one draw needn't show every extreme that they name: `slot_token`: within one device the 96 slots name distinct tokens of that device. `slot_count`: at least one device has all 96 slots live.
All inputs are finite; a program needn't handle non-finite values.
Results may differ from a plain program's by a relative error of at most 0.001.
Values may be sent and summed in bfloat16 or wider, within the bound.
No kernel may reach another device: no remote copies, remote signals or barrier semaphores. Data moves between devices by JAX's collectives and lax.ppermute only.
A program may use at most 192 MiB of HBM per device.

v0:
```python
import jax
import jax.numpy as jnp
from jax import lax
from jax.sharding import PartitionSpec as P


def adamw(grad, master, moment, second):
    corr_one = 1.0 - 0.9**20
    corr_two = 1.0 - 0.95**20
    new_moment = 0.9 * moment + 0.1 * grad
    new_second = 0.95 * second + 0.05 * grad * grad
    step_dir = new_moment / corr_one / (jnp.sqrt(new_second / corr_two) + 1e-08)
    new_master = master - 0.02 * (step_dir + 0.1 * master)
    return (new_moment, new_second, new_master.astype(jnp.bfloat16))


def block_rows(activ, other, rows, groups):
    count_rows = activ.shape[0]
    grid = activ.reshape(count_rows, groups, -1, rows)
    return jnp.einsum("ngkr,nd->kgrd", grid, other, preferred_element_type=jnp.float32)


def make_term(activs, others, row_list, groups):
    share = groups * sum(row_list)

    def term(start, count):
        blocks = count // share
        pieces = [block_rows(a, o, r, groups) for a, o, r in zip(activs, others, row_list)]
        joined = pieces[0]
        return joined.reshape(blocks * share, joined.shape[3])

    return term


def local(
    hid_shared,
    hid_routed,
    out_grad,
    slot_token,
    slot_count,
    master_shared,
    moment_shared,
    second_shared,
    master_routed,
    moment_routed,
    second_routed,
):
    cut_count = lax.axis_size("cuts")
    shared_rows = master_shared.shape[0]
    routed_rows = master_routed.shape[0]
    slot_total = hid_routed.shape[0]
    live = lax.iota(jnp.int32, slot_total) < slot_count[0]
    live_act = jnp.where(live[:, None], hid_routed, jnp.zeros_like(hid_routed))
    slot_grad = out_grad[slot_token]
    term_shared = make_term((hid_shared,), (out_grad,), (shared_rows,), cut_count)
    term_routed = make_term((live_act,), (slot_grad,), (routed_rows,), cut_count)
    within_shared = lax.psum_scatter(
        term_shared(jnp.int32(0), lax.axis_size("fsdp") * (cut_count * shared_rows)),
        "fsdp",
        scatter_dimension=0,
        tiled=True,
    )
    within_routed = lax.psum_scatter(
        term_routed(jnp.int32(0), lax.axis_size("fsdp") * (cut_count * routed_rows)),
        "fsdp",
        scatter_dimension=0,
        tiled=True,
    )
    grad_shared, grad_routed = (
        lax.psum_scatter(within_shared, "cuts", scatter_dimension=0, tiled=True),
        lax.psum_scatter(within_routed, "cuts", scatter_dimension=0, tiled=True),
    )
    moment_s, second_s, weight_s = adamw(grad_shared, master_shared, moment_shared, second_shared)
    moment_r, second_r, weight_r = adamw(grad_routed, master_routed, moment_routed, second_routed)
    full_shared, full_routed = (
        lax.all_gather(weight_s, "fsdp", axis=0, tiled=True),
        lax.all_gather(weight_r, "fsdp", axis=0, tiled=True),
    )
    return (moment_s, second_s, moment_r, second_r, full_shared, full_routed)


def solution(mesh):
    placed = (
        P(("cuts", "fsdp"), None),
        P(("cuts", "fsdp"), None),
        P(("cuts", "fsdp"), None),
        P(("cuts", "fsdp")),
        P(("cuts", "fsdp")),
        P(("cuts", "fsdp"), None),
        P(("cuts", "fsdp"), None),
        P(("cuts", "fsdp"), None),
        P(("cuts", "fsdp"), None),
        P(("cuts", "fsdp"), None),
        P(("cuts", "fsdp"), None),
    )
    return jax.shard_map(
        local,
        mesh=mesh,
        in_specs=placed,
        out_specs=(
            P(("cuts", "fsdp"), None),
            P(("cuts", "fsdp"), None),
            P(("cuts", "fsdp"), None),
            P(("cuts", "fsdp"), None),
            P("cuts", None),
            P("cuts", None),
        ),
        check_vma=False,
    )
```

profile of v0, /device:TPU:16, one launch (start us, length us, event | category | flops | bytes accessed | tf_op | source)
XLA Modules:
  0.0 826.0 jit_solution(4092189958343732047)
XLA Ops:
  8.0 2.8 copy.25
  10.9 2.5 reshape.28
  13.4 10.1 %convolution_bitcast_fusion = f32[64,4,6,2560]{3,0,2,1:T(8,128)S(1)} fusion(bf16[768,2560]{1,0:T(8,128)(2,1)} %param.13, bf16[768,4,64,6]{0,3,2,1:T(8,128)(2,1)} %reshape.28), kind=kOutput, calls=%fused_computation.1 | convolution fusion | flops 6039797760 | bytes 22020096 | tf_op jit(solution)/shard_map/ngkr,nd->kgrd/dot_general | solution.py:20
  23.4 14.3 %copy.27 = f32[64,4,6,2560]{3,2,1,0:T(8,128)} copy(f32[64,4,6,2560]{3,0,2,1:T(8,128)S(1)} %convolution_bitcast_fusion) | data formatting | bytes 31457280 | tf_op jit(solution)/shard_map/ngkr,nd->kgrd/transpose | solution.py:20
  37.7 18.4 %reshape.29 = f32[1536,2560]{1,0:T(8,128)} reshape(f32[64,4,6,2560]{3,2,1,0:T(8,128)} %copy.27) | data formatting | bytes 31457280 | tf_op jit(solution)/shard_map/reshape | solution.py:30
  56.4 0.4 copy-done.16
  56.8 4.0 gather_fusion
  61.8 4.3 convolution_bitcast_fusion.1
  66.2 12.6 %copy.30 = f32[64,4,3,2560]{3,2,1,0:T(4,128)} copy(f32[64,4,3,2560]{3,0,2,1:T(8,128)} %convolution_bitcast_fusion.1) | data formatting | bytes 15728640 | tf_op jit(solution)/shard_map/ngkr,nd->kgrd/transpose | solution.py:20
  78.8 12.7 %reshape.31 = f32[768,2560]{1,0:T(8,128)} reshape(f32[64,4,3,2560]{3,2,1,0:T(4,128)} %copy.30) | data formatting | bytes 15728640 | tf_op jit(solution)/shard_map/reshape | solution.py:30
  91.5 228.3 %fusion.1 = f32[16,2560]{1,0:T(8,128)S(1)} fusion(f32[768,2560]{1,0:T(8,128)} %reshape.31), kind=kCustom, calls=%all-reduce-scatter.1 | all-reduce-scatter fusion | flops 2621441 | bytes 8029184
  319.9 8.9 %collective-permute-start.16 = (f32[12,2560]{1,0:T(8,128)S(1)}, f32[12,2560]{1,0:T(8,128)S(1)}, u32[]{:S(2)}, u32[]{:S(2)}) collective-permute-start(f32[12,2560]{1,0:T(8,128)S(1)} %slice.3), channel_id=1, source_target_pairs={{0,16},{1,17},{2,18},{3,19},{4,20},{5,21},{6,22},{7,23},{8,24},{9,... | collective-permute-start | bytes 368648
  328.8 1.3 collective-permute-start.15
  330.1 7.7 collective-permute-start.14
  337.8 2.1 collective-permute-start.13
  339.9 5.1 collective-permute-start.12
  345.0 4.9 collective-permute-start.11
  349.9 0.6 collective-permute-done.15
  350.6 7.1 collective-permute-start.10
  357.7 3.9 collective-permute-done.14
  361.5 1.3 collective-permute-start.9
  362.8 7.7 collective-permute-done.13
  370.5 6.8 collective-permute-start.8
  377.4 1.3 collective-permute-start.7
  378.7 2.6 collective-permute-done.11
  381.3 9.2 %collective-permute-start.6 = (f32[16,2560]{1,0:T(8,128)S(1)}, f32[16,2560]{1,0:T(8,128)S(1)}, u32[]{:S(2)}, u32[]{:S(2)}) collective-permute-start(f32[16,2560]{1,0:T(8,128)S(1)} %fusion.1), channel_id=1, source_target_pairs={{0,6},{1,7},{2,8},{3,9},{4,10},{5,11},{6,12},{7,13},{8,14},{9,15},... | collective-permute-start | bytes 491528
  390.5 8.6 %collective-permute-start.5 = (f32[16,2560]{1,0:T(8,128)S(1)}, f32[16,2560]{1,0:T(8,128)S(1)}, u32[]{:S(2)}, u32[]{:S(2)}) collective-permute-start(f32[16,2560]{1,0:T(8,128)S(1)} %fusion.1), channel_id=1, source_target_pairs={{0,5},{1,6},{2,7},{3,8},{4,9},{5,10},{6,11},{7,12},{8,13},{9,14},{... | collective-permute-start | bytes 491528
  399.1 4.7 collective-permute-start.4
  403.7 0.9 collective-permute-done.8
  404.6 42.7 %collective-permute-start.3 = (f32[16,2560]{1,0:T(8,128)S(1)}, f32[16,2560]{1,0:T(8,128)S(1)}, u32[]{:S(2)}, u32[]{:S(2)}) collective-permute-start(f32[16,2560]{1,0:T(8,128)S(1)} %fusion.1), channel_id=1, source_target_pairs={{0,3},{1,4},{2,5},{3,6},{4,7},{5,8},{6,9},{7,10},{8,11},{9,12},{10... | collective-permute-start | bytes 491528
  447.3 1.3 collective-permute-start.2
  448.7 9.2 %collective-permute-start.1 = (f32[16,2560]{1,0:T(8,128)S(1)}, f32[16,2560]{1,0:T(8,128)}, u32[]{:S(2)}, u32[]{:S(2)}) collective-permute-start(f32[16,2560]{1,0:T(8,128)S(1)} %fusion.1), channel_id=1, source_target_pairs={{0,1},{1,2},{2,3},{3,4},{4,5},{5,6},{6,7},{7,8},{8,9},{9,10},{10,1... | collective-permute-start | bytes 491528
  458.0 0.6 dynamic-slice.12
  458.6 0.6 fusion.12
  460.5 0.6 copy-done.8
  461.3 0.7 copy-done.11
  461.9 14.3 %concatenate.1 = f32[268,2560]{1,0:T(8,128)S(1)} concatenate(f32[12,2560]{1,0:T(8,128)S(1)} %collective-permute-done.16, f32[16,2560]{1,0:T(8,128)S(1)} %collective-permute-done.15, f32[16,2560]{1,0:T(8,128)S(1)} %collective-permute-done.14, f32[16,2560]{1,0:T(8,128)} %copy-done, f32[16,2560]{1,0:T(8,128)} %copy-done.1, f32[16,2560]{1,0:T(8,128)} %copy-done.2, ...), dimensions={0} | concatenate | bytes 5488640
  476.3 11.8 %fusion = f32[8,2560]{1,0:T(8,128)S(1)} fusion(f32[24,2560]{1,0:T(8,128)} %reduce-scatter.6.cloned.1.call-done), kind=kCustom, calls=%all-reduce-scatter | all-reduce-scatter fusion | flops 81921 | bytes 328704
  488.1 1.9 collective-permute-start
  490.0 0.7 constant_dynamic-slice_fusion
  490.8 4.9 collective-permute-done
  495.8 1.6 fusion.8
  498.1 51.5 %all-reduce.7.cloned.1.call-done = f32[12,2560]{1,0:T(8,128)} async-done(((f32[12,2560]{1,0:T(8,128)}), f32[12,2560]{1,0:T(8,128)}) %all-reduce.7.cloned.1.call-update) | async-done | bytes 122896
  549.7 1.6 fusion.9
  551.3 165.2 %all-gather.1 = bf16[64,3,2560]{2,1,0:T(4,128)(2,1)S(1)} all-gather(bf16[1,3,2560]{2,1,0:T(4,128)(2,1)S(1)} %get-tuple-element.6), channel_id=1, replica_groups=mesh['cuts'=4,'fsdp'=64] {'fsdp'}, dimensions={0}, use_global_device_ids=true | all-gather | bytes 998400 | tf_op jit(solution)/shard_map/all_gather | solution.py:77
  716.5 1.6 reshape.44
  718.1 96.4 %all-gather.4.cloned.1.call-done = bf16[64,6,2560]{2,1,0:T(8,128)(2,1)} async-done(((bf16[1,6,2560]{2,1,0:T(8,128)(2,1)}), bf16[64,6,2560]{2,1,0:T(8,128)(2,1)}) %all-gather.4.cloned.1.call-update) | async-done | bytes 1966096 | tf_op jit(solution)/shard_map/all_gather | solution.py:76
  814.5 4.1 reshape.42
  (58 shorter events, 1.2 us)
Async XLA Ops:
  8.0 468.2 %reduce-scatter.6.cloned.1.call-start = ((), (), s32[]{:S(2)}) async-start(), calls=%async_computation.1 | async-start | bytes 15974400 | tf_op jit(solution)/shard_map/reduce_scatter | solution.py:57
  56.1 0.7 copy-start.16
  56.2 5.3 copy-start.12
  56.2 493.5 %all-reduce.7.cloned.1.call-start = ((), (), s32[]{:S(2)}) async-start(), calls=%async_computation.3 | async-start | bytes 327680
  91.5 366.5 %copy-start.15 = (u32[256]{0:T(256)S(1)}, u32[256]{0:T(256)}, u32[]{:S(2)}) copy-start(u32[256]{0:T(256)} %constant.49) | copy-start | bytes 3076
  91.5 367.1 %copy-start.14 = (u32[256]{0:T(256)S(1)}, u32[256]{0:T(256)}, u32[]{:S(2)}) copy-start(u32[256]{0:T(256)} %constant.45) | copy-start | bytes 3076
  319.8 176.0 %copy-start.13 = (f32[6,2560]{1,0:T(8,128)S(1)}, f32[6,2560]{1,0:T(8,128)}, u32[]{:S(2)}) copy-start(f32[6,2560]{1,0:T(8,128)} %param.16) | copy-start | bytes 184324
  319.9 25.2 %collective-permute-start.16 = (f32[12,2560]{1,0:T(8,128)S(1)}, f32[12,2560]{1,0:T(8,128)S(1)}, u32[]{:S(2)}, u32[]{:S(2)}) collective-permute-start(f32[12,2560]{1,0:T(8,128)S(1)} %slice.3), channel_id=1, source_target_pairs={{0,16},{1,17},{2,18},{3,19},{4,20},{5,21},{6,22},{7,23},{8,24},{9,... | collective-permute-start | bytes 368648
  328.8 21.8 %collective-permute-start.15 = (f32[16,2560]{1,0:T(8,128)S(1)}, f32[16,2560]{1,0:T(8,128)S(1)}, u32[]{:S(2)}, u32[]{:S(2)}) collective-permute-start(f32[16,2560]{1,0:T(8,128)S(1)} %fusion.1), channel_id=1, source_target_pairs={{0,15},{1,16},{2,17},{3,18},{4,19},{5,20},{6,21},{7,22},{8,23},{9,... | collective-permute-start | bytes 491528
  330.1 31.4 %collective-permute-start.14 = (f32[16,2560]{1,0:T(8,128)S(1)}, f32[16,2560]{1,0:T(8,128)S(1)}, u32[]{:S(2)}, u32[]{:S(2)}) collective-permute-start(f32[16,2560]{1,0:T(8,128)S(1)} %fusion.1), channel_id=1, source_target_pairs={{0,14},{1,15},{2,16},{3,17},{4,18},{5,19},{6,20},{7,21},{8,22},{9,... | collective-permute-start | bytes 491528
  337.8 32.7 %collective-permute-start.13 = (f32[16,2560]{1,0:T(8,128)S(1)}, f32[16,2560]{1,0:T(8,128)S(1)}, u32[]{:S(2)}, u32[]{:S(2)}) collective-permute-start(f32[16,2560]{1,0:T(8,128)S(1)} %fusion.1), channel_id=1, source_target_pairs={{0,13},{1,14},{2,15},{3,16},{4,17},{5,18},{6,19},{7,20},{8,21},{9,... | collective-permute-start | bytes 491528
  339.9 37.4 %collective-permute-start.12 = (f32[16,2560]{1,0:T(8,128)S(1)}, f32[16,2560]{1,0:T(8,128)S(1)}, u32[]{:S(2)}, u32[]{:S(2)}) collective-permute-start(f32[16,2560]{1,0:T(8,128)S(1)} %fusion.1), channel_id=1, source_target_pairs={{0,12},{1,13},{2,14},{3,15},{4,16},{5,17},{6,18},{7,19},{8,20},{9,... | collective-permute-start | bytes 491528
  345.0 36.2 %collective-permute-start.11 = (f32[16,2560]{1,0:T(8,128)S(1)}, f32[16,2560]{1,0:T(8,128)S(1)}, u32[]{:S(2)}, u32[]{:S(2)}) collective-permute-start(f32[16,2560]{1,0:T(8,128)S(1)} %fusion.1), channel_id=1, source_target_pairs={{0,11},{1,12},{2,13},{3,14},{4,15},{5,16},{6,17},{7,18},{8,19},{9,... | collective-permute-start | bytes 491528
  350.6 39.9 %collective-permute-start.10 = (f32[16,2560]{1,0:T(8,128)S(1)}, f32[16,2560]{1,0:T(8,128)S(1)}, u32[]{:S(2)}, u32[]{:S(2)}) collective-permute-start(f32[16,2560]{1,0:T(8,128)S(1)} %fusion.1), channel_id=1, source_target_pairs={{0,10},{1,11},{2,12},{3,13},{4,14},{5,15},{6,16},{7,17},{8,18},{9,... | collective-permute-start | bytes 491528
  361.5 37.5 %collective-permute-start.9 = (f32[16,2560]{1,0:T(8,128)S(1)}, f32[16,2560]{1,0:T(8,128)S(1)}, u32[]{:S(2)}, u32[]{:S(2)}) collective-permute-start(f32[16,2560]{1,0:T(8,128)S(1)} %fusion.1), channel_id=1, source_target_pairs={{0,9},{1,10},{2,11},{3,12},{4,13},{5,14},{6,15},{7,16},{8,17},{9,1... | collective-permute-start | bytes 491528
  370.5 78.2 %copy-start = (f32[16,2560]{1,0:T(8,128)}, f32[16,2560]{1,0:T(8,128)S(1)}, u32[]{:S(2)}) copy-start(f32[16,2560]{1,0:T(8,128)S(1)} %collective-permute-done.13) | copy-start | bytes 491524
  370.5 34.1 %collective-permute-start.8 = (f32[16,2560]{1,0:T(8,128)S(1)}, f32[16,2560]{1,0:T(8,128)S(1)}, u32[]{:S(2)}, u32[]{:S(2)}) collective-permute-start(f32[16,2560]{1,0:T(8,128)S(1)} %fusion.1), channel_id=1, source_target_pairs={{0,8},{1,9},{2,10},{3,11},{4,12},{5,13},{6,14},{7,15},{8,16},{9,17... | collective-permute-start | bytes 491528
  377.4 80.6 %copy-start.1 = (f32[16,2560]{1,0:T(8,128)}, f32[16,2560]{1,0:T(8,128)S(1)}, u32[]{:S(2)}) copy-start(f32[16,2560]{1,0:T(8,128)S(1)} %collective-permute-done.12) | copy-start | bytes 491524
  377.4 69.9 %collective-permute-start.7 = (f32[16,2560]{1,0:T(8,128)S(1)}, f32[16,2560]{1,0:T(8,128)S(1)}, u32[]{:S(2)}, u32[]{:S(2)}) collective-permute-start(f32[16,2560]{1,0:T(8,128)S(1)} %fusion.1), channel_id=1, source_target_pairs={{0,7},{1,8},{2,9},{3,10},{4,11},{5,12},{6,13},{7,14},{8,15},{9,16}... | collective-permute-start | bytes 491528
  381.3 76.7 %copy-start.2 = (f32[16,2560]{1,0:T(8,128)}, f32[16,2560]{1,0:T(8,128)S(1)}, u32[]{:S(2)}) copy-start(f32[16,2560]{1,0:T(8,128)S(1)} %collective-permute-done.11) | copy-start | bytes 491524
  381.3 67.4 %collective-permute-start.6 = (f32[16,2560]{1,0:T(8,128)S(1)}, f32[16,2560]{1,0:T(8,128)S(1)}, u32[]{:S(2)}, u32[]{:S(2)}) collective-permute-start(f32[16,2560]{1,0:T(8,128)S(1)} %fusion.1), channel_id=1, source_target_pairs={{0,6},{1,7},{2,8},{3,9},{4,10},{5,11},{6,12},{7,13},{8,14},{9,15},... | collective-permute-start | bytes 491528
  390.4 67.5 %copy-start.3 = (f32[16,2560]{1,0:T(8,128)}, f32[16,2560]{1,0:T(8,128)S(1)}, u32[]{:S(2)}) copy-start(f32[16,2560]{1,0:T(8,128)S(1)} %collective-permute-done.10) | copy-start | bytes 491524
  390.5 70.0 %collective-permute-start.5 = (f32[16,2560]{1,0:T(8,128)S(1)}, f32[16,2560]{1,0:T(8,128)S(1)}, u32[]{:S(2)}, u32[]{:S(2)}) collective-permute-start(f32[16,2560]{1,0:T(8,128)S(1)} %fusion.1), channel_id=1, source_target_pairs={{0,5},{1,6},{2,7},{3,8},{4,9},{5,10},{6,11},{7,12},{8,13},{9,14},{... | collective-permute-start | bytes 491528
  399.0 58.9 %copy-start.4 = (f32[16,2560]{1,0:T(8,128)}, f32[16,2560]{1,0:T(8,128)S(1)}, u32[]{:S(2)}) copy-start(f32[16,2560]{1,0:T(8,128)S(1)} %collective-permute-done.9) | copy-start | bytes 491524
  399.1 61.4 %collective-permute-start.4 = (f32[16,2560]{1,0:T(8,128)S(1)}, f32[16,2560]{1,0:T(8,128)S(1)}, u32[]{:S(2)}, u32[]{:S(2)}) collective-permute-start(f32[16,2560]{1,0:T(8,128)S(1)} %fusion.1), channel_id=1, source_target_pairs={{0,4},{1,5},{2,6},{3,7},{4,8},{5,9},{6,10},{7,11},{8,12},{9,13},{1... | collective-permute-start | bytes 491528
  404.6 53.3 %copy-start.5 = (f32[16,2560]{1,0:T(8,128)}, f32[16,2560]{1,0:T(8,128)S(1)}, u32[]{:S(2)}) copy-start(f32[16,2560]{1,0:T(8,128)S(1)} %collective-permute-done.8) | copy-start | bytes 491524
  404.6 55.9 %collective-permute-start.3 = (f32[16,2560]{1,0:T(8,128)S(1)}, f32[16,2560]{1,0:T(8,128)S(1)}, u32[]{:S(2)}, u32[]{:S(2)}) collective-permute-start(f32[16,2560]{1,0:T(8,128)S(1)} %fusion.1), channel_id=1, source_target_pairs={{0,3},{1,4},{2,5},{3,6},{4,7},{5,8},{6,9},{7,10},{8,11},{9,12},{10... | collective-permute-start | bytes 491528
  447.3 10.6 %copy-start.6 = (f32[16,2560]{1,0:T(8,128)}, f32[16,2560]{1,0:T(8,128)S(1)}, u32[]{:S(2)}) copy-start(f32[16,2560]{1,0:T(8,128)S(1)} %collective-permute-done.7) | copy-start | bytes 491524
  447.3 13.2 %collective-permute-start.2 = (f32[16,2560]{1,0:T(8,128)S(1)}, f32[16,2560]{1,0:T(8,128)S(1)}, u32[]{:S(2)}, u32[]{:S(2)}) collective-permute-start(f32[16,2560]{1,0:T(8,128)S(1)} %fusion.1), channel_id=1, source_target_pairs={{0,2},{1,3},{2,4},{3,5},{4,6},{5,7},{6,8},{7,9},{8,10},{9,11},{10,... | collective-permute-start | bytes 491528
  448.7 9.3 %copy-start.7 = (f32[16,2560]{1,0:T(8,128)}, f32[16,2560]{1,0:T(8,128)S(1)}, u32[]{:S(2)}) copy-start(f32[16,2560]{1,0:T(8,128)S(1)} %collective-permute-done.6) | copy-start | bytes 491524
  448.7 13.3 %collective-permute-start.1 = (f32[16,2560]{1,0:T(8,128)S(1)}, f32[16,2560]{1,0:T(8,128)}, u32[]{:S(2)}, u32[]{:S(2)}) collective-permute-start(f32[16,2560]{1,0:T(8,128)S(1)} %fusion.1), channel_id=1, source_target_pairs={{0,1},{1,2},{2,3},{3,4},{4,5},{5,6},{6,7},{7,8},{8,9},{9,10},{10,1... | collective-permute-start | bytes 491528
  460.5 0.7 copy-start.8
  460.5 0.7 copy-start.9
  460.5 0.8 copy-start.10
  461.3 0.7 copy-start.11
  488.1 7.6 collective-permute-start
  490.7 323.8 %all-gather.4.cloned.1.call-start = ((), (), s32[]{:S(2)}) async-start(), calls=%async_computation.2 | async-start | bytes 2662400 | tf_op jit(solution)/shard_map/all_gather | solution.py:76
Sparse Core Ops, SparseCore 0:
  56.3 416.1 reduce-scatter.5
  497.6 316.8 all-gather.3
Sparse Core Ops, SparseCore 1:
  490.8 58.8 all-reduce.6
where the time goes:
time: 828 us; the launch traced here: 826 us
  blocking collectives  405 us (49%)
  waiting for transfers between devices  169 us (20%)
  starting transfers between devices  124 us (15%)
  local copies, waits for them, and re-layouts  91.5 us (11%)
  between operations  18.6 us (2%)
  matrix products  14.4 us (2%)
    unnamed x2, blocking collectives  240 us
    all_gather x1, blocking collectives, local(): lax.all_gather(weight_r, 'fsdp', axis=0, tiled=True)  165 us
    unnamed x18, starting transfers between devices  124 us
    all_gather x1, waiting for transfers between devices, local(): lax.all_gather(weight_s, 'fsdp', axis=0, tiled=True)  96.4 us
    unnamed x21, waiting for transfers between devices  72.2 us
    reshape x2, local copies, waits for them, and re-layouts, term(): return joined.reshape(blocks * share, joined.shape[3])  31.1 us
    transpose x2, local copies, waits for them, and re-layouts, block_rows(): jnp.einsum('ngkr,nd->kgrd', grid, other, preferred_element_type=jnp.float32)  26.9 us
    unnamed x44, local copies, waits for them, and re-layouts  26.7 us
  transfers between devices with their start and end apart: 20, of which 8 were waited for; matrix products, arithmetic and copies ran while one was open for 34% of the time, Pallas kernels for 0%

commit v1 on v0

v1 whole, which is shorter than its diff:
```python
import jax
import jax.numpy as jnp
import numpy as np
from jax import lax
from jax.sharding import Mesh, PartitionSpec as P

AXES = ("yh", "core", "yl", "z", "x")
NX, NY, NZ = 4, 4, 8
SCALE = 0.25
BF = jnp.bfloat16
F32 = jnp.float32
F16 = jnp.float16


def adamw(grad, master, moment, second):
    corr_one = 1.0 - 0.9**20
    corr_two = 1.0 - 0.95**20
    new_moment = 0.9 * moment + 0.1 * grad
    new_second = 0.95 * second + 0.05 * grad * grad
    step_dir = new_moment / corr_one / (jnp.sqrt(new_second / corr_two) + 1e-08)
    new_master = master - 0.02 * (step_dir + 0.1 * master)
    return (new_moment, new_second, new_master.astype(BF))


def x_ring(v, d):
    return lax.ppermute(v, "x", [(i, (i + d) % NX) for i in range(NX)])


def y_ring(v, d):
    return lax.ppermute(v, ("yh", "yl"), [(i, (i + d) % NY) for i in range(NY)])


def core_swap(v):
    return lax.ppermute(v, "core", [(0, 1), (1, 0)])


def row_order(sr, rr):
    rows = sr + rr
    n = NX * NY * NZ * rows
    xs, ys, zs, i = np.meshgrid(np.arange(NX), np.arange(NY), np.arange(NZ), np.arange(rows), indexing="ij")
    dev = ((ys % 2) * NZ + zs) * NX + xs
    shared = np.zeros((n, 2 * 2 * NZ * NX * sr), np.float32)
    flat = np.arange(n)
    col = ((ys // 2) * (2 * NZ * NX) + dev) * sr + i
    keep = (i < sr).reshape(-1)
    shared[flat[keep], col.reshape(-1)[keep]] = 1
    routed = []
    for core in range(2):
        one = np.zeros((n, 4 * 2 * NZ * NX * rr), np.float32)
        col = (((ys // 2) * 2 + core) * (2 * NZ * NX) + dev) * rr + i - sr
        one[flat[~keep], col.reshape(-1)[~keep]] = 1
        routed.append(one)
    return shared.astype(jnp.bfloat16), np.stack(routed).astype(jnp.bfloat16)


def dot_t(a, b):
    return lax.dot_general(a, b, (((1,), (1,)), ((), ())), preferred_element_type=F32)


def dot(a, b):
    return jnp.dot(a, b, preferred_element_type=F32)


def local(
    hid_shared,
    hid_routed,
    out_grad,
    slot_token,
    slot_count,
    master_shared,
    moment_shared,
    second_shared,
    master_routed,
    moment_routed,
    second_routed,
):
    tok, width = out_grad.shape
    slots = hid_routed.shape[0]
    sr, rr = master_shared.shape[0], master_routed.shape[0]
    rows = sr + rr
    half = width // 2
    cut = hid_shared.shape[1] // 4
    core = lax.axis_index("core")
    x = lax.axis_index("x")
    yh, yl = lax.axis_index("yh"), lax.axis_index("yl")
    y = yh * 2 + yl

    shared_order, routed_order = row_order(sr, rr)
    shared_order = jnp.asarray(shared_order)
    routed_order = jnp.asarray(routed_order)
    live = lax.iota(jnp.int32, slots) < slot_count[0]
    place = (slot_token[:, None] == lax.broadcasted_iota(jnp.int32, (slots, tok), 1)) & live[:, None]
    place = place.astype(BF)

    def activ(k):
        cols = [lax.dynamic_slice(hid_shared, (0, (h * 2 + k) * cut), (tok, cut)) for h in range(2)]
        one = dot_t(shared_order, jnp.concatenate(cols, axis=1))
        order = lax.dynamic_index_in_dim(routed_order, k, 0, keepdims=False)
        two = dot(dot_t(order, hid_routed).astype(BF), place)
        return (one + two).astype(BF)

    og = (out_grad[:, :half], out_grad[:, half:])
    og_far = [None, None]
    og_far[0] = core_swap(og[0])
    act_far = core_swap(activ(1 - core))
    og_far[1] = core_swap(og[1])
    act_near = activ(core)

    group = NZ * rows
    act_near = act_near.reshape(NX, NY, group, tok)
    act_far = act_far.reshape(NX, NY, group, tok)

    def term(part, dim, index):
        def pick(a):
            return lax.dynamic_index_in_dim(a, index, dim, keepdims=False).reshape(-1, tok)

        total = dot(pick(act_near), og[part]) + dot(pick(act_far), og_far[part])
        return SCALE * total

    rings = (x_ring, y_ring)
    place_of = (x, y)
    firsts = []
    for part in range(2):
        ring, me = rings[part], place_of[part]
        got = [ring(term(part, part, (me + d) % 4).astype(F16), d) for d in (2, 1, 3)]
        total = term(part, part, me)
        for g in got:
            total = total + g.astype(F32)
        firsts.append(total.reshape(4, group, half))
    seconds = []
    for part in range(2):
        ring, me = rings[1 - part], place_of[1 - part]

        def pick(index):
            return lax.dynamic_index_in_dim(firsts[part], index, 0, keepdims=False)

        got = [ring(pick((me + d) % 4).astype(F16), d) for d in (2, 1, 3)]
        total = pick(me)
        for g in got:
            total = total + g.astype(F32)
        seconds.append(total.astype(F16))
    last = jnp.concatenate(seconds, axis=1).reshape(NZ, rows * width // 128, 128)
    last = lax.all_to_all(last, "z", 0, 0)
    grad = (last.astype(F32).sum(axis=0) * (1.0 / SCALE)).reshape(rows, width)

    moment_s, second_s, weight_s = adamw(grad[:sr], master_shared, moment_shared, second_shared)
    moment_r, second_r, weight_r = adamw(grad[sr:], master_routed, moment_routed, second_routed)

    weight = jnp.concatenate([weight_s, weight_r], axis=0).reshape(rows * width // 128, 128)
    by_z = lax.all_gather(weight, "z", axis=0, tiled=False).reshape(NZ * rows, width)
    by_y = lax.ppermute(by_z, "yl", [(0, 1), (1, 0)])
    mine = jnp.concatenate([by_z, by_y], axis=0)
    full = jnp.concatenate([mine] + [x_ring(mine, d) for d in (1, 2, 3)], axis=0)

    def final(count, low, outer):
        r = lax.broadcasted_iota(jnp.int32, (outer, full.shape[0]), 0)
        q = lax.broadcasted_iota(jnp.int32, (outer, full.shape[0]), 1)
        i = r % count
        xx = (r // count) % NX
        zz = (r // (count * NX)) % NZ
        yy = r // (count * NX * NZ)
        back = (x - xx) % NX
        flip = yy ^ yl
        want = ((back * 2 + flip) * NZ + zz) * rows + low + i
        return dot((q == want).astype(BF), full).astype(BF)

    n = 2 * NZ * NX
    return (moment_s, second_s, moment_r, second_r, final(sr, 0, n * sr), final(rr, sr, n * rr))


def solution(mesh):
    fine = Mesh(mesh.devices.reshape(2, 2, 2, NZ, NX), AXES)
    split = P(AXES, None)
    flat = P(AXES)
    cuts = P(("yh", "core"), None)
    return jax.shard_map(
        local,
        mesh=fine,
        in_specs=(split, split, split, flat, flat) + (split,) * 6,
        out_specs=(split,) * 4 + (cuts,) * 2,
        check_vma=False,
    )
```

time: 828 us -> 200 us (0.24)
  blocking collectives: 405 us -> 25.2 us
  waiting for transfers between devices: 169 us -> 74.8 us
  starting transfers between devices: 124 us -> 31.2 us
  local copies, waits for them, and re-layouts: 91.5 us -> 13.2 us
  matrix products: 14.4 us -> 51.2 us
  between operations: 18.6 us -> 1.98 us
    unnamed x2 -> x0, blocking collectives: 240 us -> none
    all_gather x1, blocking collectives: 165 us -> 25.2 us  [local(): lax.all_gather(weight, 'z', axis=0, tiled=False).reshape(NZ * rows, width)]
    unnamed x18 -> x0, starting transfers between devices: 124 us -> none
    all_gather x1 -> x0, waiting for transfers between devices: 96.4 us -> none  [local(): lax.all_gather(weight_s, 'fsdp', axis=0, tiled=True)]
    unnamed x21 -> x0, waiting for transfers between devices: 72.2 us -> none
    ppermute x0 -> x19, waiting for transfers between devices: none -> 60.5 us  [the longest x9 46.2 us: x_ring(): return lax.ppermute(v, 'x', [(i, (i + d) % NX) for i in range(NX)])]
    dot_general x2 -> x24, matrix products: 14.4 us -> 51.2 us  [the longest x20 40.7 us: dot(): return jnp.dot(a, b, preferred_element_type=F32)]
    reshape x4 -> x2, local copies, waits for them, and re-layouts: 33.7 us -> 1.63 us  [the longest x1 1.21 us: local(): jnp.concatenate(seconds, axis=1).reshape(NZ, rows * width // 128, 128)]
  transfers between devices with their start and end apart: 20 -> 20, of which waited for: 8 -> 11; matrix products, arithmetic and copies ran while one was open for 34% -> 21% of each run, Pallas kernels for 0% -> 0%
where the time goes in v1:
time: 200 us
  waiting for transfers between devices  74.8 us (37%)
  matrix products  51.2 us (26%)
  starting transfers between devices  31.2 us (16%)
  blocking collectives  25.2 us (13%)
  local copies, waits for them, and re-layouts  13.2 us (7%)
  other arithmetic  2.14 us (1%)
    ppermute x9, waiting for transfers between devices, x_ring(): return lax.ppermute(v, 'x', [(i, (i + d) % NX) for i in range(NX)])  46.2 us
    dot_general x20, matrix products, dot(): return jnp.dot(a, b, preferred_element_type=F32)  40.7 us
    all_gather x1, blocking collectives, local(): lax.all_gather(weight, 'z', axis=0, tiled=False).reshape(NZ * rows, width)  25.2 us
    all_to_all x1, waiting for transfers between devices, local(): last = lax.all_to_all(last, 'z', 0, 0)  14.3 us
    ppermute x9, starting transfers between devices, x_ring(): return lax.ppermute(v, 'x', [(i, (i + d) % NX) for i in range(NX)])  13.3 us
    dot_general x4, matrix products, dot_t(): lax.dot_general(a, b, (((1,), (1,)), ((), ())), preferred_element_type=F32)  10.6 us
    all_to_all x1, starting transfers between devices, local(): last = lax.all_to_all(last, 'z', 0, 0)  8.47 us
    ppermute x6, waiting for transfers between devices, y_ring(): return lax.ppermute(v, ('yh', 'yl'), [(i, (i + d) % NY) for i in range(NY)])  8.16 us
  transfers between devices with their start and end apart: 20, of which 11 were waited for; matrix products, arithmetic and copies ran while one was open for 21% of the time, Pallas kernels for 0%

profile of v1, /device:TPU:16, one launch (start us, length us, event | category | flops | bytes accessed | tf_op | source)
XLA Modules:
  0.0 199.7 jit_solution(12508809407896078693)
XLA Ops:
  1.5 0.9 copy-done
  2.3 2.4 %fusion.54 = f32[768,1152]{1,0:T(8,128)S(1)} fusion(bf16[1152,384]{1,0:T(8,128)(2,1)} %constant.284, bf16[768,1536]{1,0:T(8,128)(2,1)S(1)} %copy-done, s32[]{:T(128)S(6)} %select_n.163), kind=kOutput, calls=%fused_computation.92 | convolution fusion | flops 679477248 | bytes 5013508 | tf_op jit(solution)/shard_map/dot_general | solution.py:57
  4.8 2.9 %fusion.1 = f32[1152,768]{0,1:T(8,128)} fusion(f32[768,1152]{1,0:T(8,128)S(1)} %fusion.54, bf16[1152,384]{1,0:T(8,128)(2,1)S(1)} %copy-done.3, bf16[768,1536]{1,0:T(8,128)(2,1)S(1)} %copy-done, s32[]{:T(128)S(6)} %select_n.164), kind=kOutput, calls=%fused_computation.6 | convolution fusion | flops 680361984 | bytes 8552452 | tf_op jit(solution)/shard_map/dot_general | solution.py:57
  7.7 4.9 %fusion.3 = bf16[1152,768]{0,1:T(8,128)(2,1)} fusion(f32[1152,768]{0,1:T(8,128)} %fusion.1, bf16[96,768]{1,0:T(8,128)(2,1)S(1)} %copy-done.4, bf16[2,1152,768]{2,1,0:T(8,128)(2,1)} %constant.274.clone, s32[]{:T(128)S(6)} %select_n.165, s32[96]{0:T(128)S(1)} %copy-done.11, pred[96]{0:T(512)(128)(4,1)S(1)} %iota_compare_fusion.1), kind=kOutput, calls=%fused_computation.9 | convolution fusion | flops 341766144 | bytes 7225828 | tf_op jit(solution)/shard_map/dot_general | solution.py:61
  12.6 4.3 %fusion.200 = (bf16[768,1280]{1,0:T(8,128)(2,1)}, bf16[768,1280]{1,0:T(8,128)(2,1)}) fusion(bf16[768,2560]{1,0:T(8,128)(2,1)} %param.15), kind=kLoop, calls=%fused_computation.296 | loop fusion | bytes 7864320 | tf_op jit(solution)/shard_map/slice | solution.py:102
  17.4 2.3 %fusion.57 = f32[768,1152]{1,0:T(8,128)S(1)} fusion(bf16[1152,384]{1,0:T(8,128)(2,1)} %constant.284, bf16[768,1536]{1,0:T(8,128)(2,1)S(1)} %copy-done, s32[]{:T(128)S(6)} %select_n.159), kind=kOutput, calls=%fused_computation.95 | convolution fusion | flops 679477248 | bytes 5013508 | tf_op jit(solution)/shard_map/dot_general | solution.py:57
  19.7 3.0 %fusion = f32[1152,768]{0,1:T(8,128)} fusion(f32[768,1152]{1,0:T(8,128)S(1)} %fusion.57, bf16[1152,384]{1,0:T(8,128)(2,1)S(1)} %copy-done.3, bf16[768,1536]{1,0:T(8,128)(2,1)S(1)} %copy-done, s32[]{:T(128)S(6)} %select_n.160), kind=kOutput, calls=%fused_computation.5 | convolution fusion | flops 680361984 | bytes 8552452 | tf_op jit(solution)/shard_map/dot_general | solution.py:57
  22.6 3.7 %fusion.2 = bf16[1152,768]{0,1:T(8,128)(2,1)S(1)} fusion(f32[1152,768]{0,1:T(8,128)} %fusion, bf16[96,768]{1,0:T(8,128)(2,1)} %param.14, bf16[2,1152,768]{2,1,0:T(8,128)(2,1)} %constant.274.clone, s32[]{:T(128)S(6)} %select_n.161, s32[96]{0:T(128)S(1)} %copy-done.11, pred[96]{0:T(512)(128)(4,1)S(1)} %iota_compare_fusion.1), kind=kOutput, calls=%fused_computation.8 | convolution fusion | flops 341766144 | bytes 7225828 | tf_op jit(solution)/shard_map/dot_general | solution.py:61
  26.4 0.9 copy.26
  27.4 2.6 %copy.28 = bf16[1152,768]{1,0:T(8,128)(2,1)S(1)} copy(bf16[1152,768]{0,1:T(8,128)(2,1)} %collective-permute-done) | data formatting | bytes 3538944 | tf_op jit(solution)/shard_map/ppermute | solution.py:34
  30.3 1.8 copy-done.2
  33.2 0.7 fusion.192
  33.9 0.7 fusion.190
  34.7 0.7 fusion.196
  35.4 0.7 fusion.186
  36.2 0.7 fusion.184
  36.9 0.7 fusion.182
  37.7 2.3 %fusion.23 = f16[288,1280]{1,0:T(8,128)(2,1)S(1)} fusion(f32[288,1280]{1,0:T(8,128)S(1)} %fusion.194, bf16[288,768]{1,0:T(8,128)(2,1)S(1)} %bitcast.112, bf16[768,1280]{1,0:T(8,128)(2,1)} %collective-permute-done.1), kind=kOutput, calls=%fused_computation.37 | convolution fusion | flops 567336960 | bytes 4620288 | tf_op jit(solution)/shard_map/dot_general | solution.py:61
  40.0 3.1 %collective-permute-start.2 = (f16[288,1280]{1,0:T(8,128)(2,1)S(1)}, f16[288,1280]{1,0:T(8,128)(2,1)S(1)}, u32[]{:S(2)}, u32[]{:S(2)}) collective-permute-start(f16[288,1280]{1,0:T(8,128)(2,1)S(1)} %fusion.23), channel_id=1, source_target_pairs={{0,2},{1,3},{2,0},{3,1},{4,6},{5,7},{6,4},{7,5},{8,10},{9,11},{10,... | collective-permute-start | bytes 2211848 | tf_op jit(solution)/shard_map/ppermute | solution.py:26
  43.1 2.3 %fusion.22 = f16[288,1280]{1,0:T(8,128)(2,1)S(1)} fusion(f32[288,1280]{1,0:T(8,128)S(1)} %fusion.192, bf16[288,768]{1,0:T(8,128)(2,1)S(1)} %bitcast.111, bf16[768,1280]{1,0:T(8,128)(2,1)} %collective-permute-done.1), kind=kOutput, calls=%fused_computation.36 | convolution fusion | flops 567336960 | bytes 4620288 | tf_op jit(solution)/shard_map/dot_general | solution.py:61
  46.1 2.3 %fusion.21 = f16[288,1280]{1,0:T(8,128)(2,1)S(1)} fusion(f32[288,1280]{1,0:T(8,128)S(1)} %fusion.190, bf16[288,768]{1,0:T(8,128)(2,1)S(1)} %bitcast.110, bf16[768,1280]{1,0:T(8,128)(2,1)} %collective-permute-done.1), kind=kOutput, calls=%fused_computation.35 | convolution fusion | flops 567336960 | bytes 4620288 | tf_op jit(solution)/shard_map/dot_general | solution.py:61
  48.4 2.7 %collective-permute-start.4 = (f16[288,1280]{1,0:T(8,128)(2,1)S(1)}, f16[288,1280]{1,0:T(8,128)(2,1)S(1)}, u32[]{:S(2)}, u32[]{:S(2)}) collective-permute-start(f16[288,1280]{1,0:T(8,128)(2,1)S(1)} %fusion.21), channel_id=1, source_target_pairs={{0,3},{1,0},{2,1},{3,2},{4,7},{5,4},{6,5},{7,6},{8,11},{9,8},{10,9... | collective-permute-start | bytes 2211848 | tf_op jit(solution)/shard_map/ppermute | solution.py:26
  51.1 2.3 %fusion.20 = f16[288,1280]{1,0:T(8,128)(2,1)S(1)} fusion(f32[288,1280]{1,0:T(8,128)S(1)} %fusion.186, bf16[288,768]{1,0:T(8,128)(2,1)S(1)} %bitcast.109, bf16[768,1280]{1,0:T(8,128)(2,1)} %collective-permute-done.8), kind=kOutput, calls=%fused_computation.34 | convolution fusion | flops 567336960 | bytes 4620288 | tf_op jit(solution)/shard_map/dot_general | solution.py:61
  54.1 2.3 %fusion.19 = f16[288,1280]{1,0:T(8,128)(2,1)S(1)} fusion(f32[288,1280]{1,0:T(8,128)S(1)} %fusion.184, bf16[288,768]{1,0:T(8,128)(2,1)S(1)} %bitcast.108, bf16[768,1280]{1,0:T(8,128)(2,1)} %collective-permute-done.8), kind=kOutput, calls=%fused_computation.33 | convolution fusion | flops 567336960 | bytes 4620288 | tf_op jit(solution)/shard_map/dot_general | solution.py:61
  56.4 2.3 %collective-permute-start.10 = (f16[288,1280]{1,0:T(8,128)(2,1)S(1)}, f16[288,1280]{1,0:T(8,128)(2,1)S(1)}, u32[]{:S(2)}, u32[]{:S(2)}) collective-permute-start(f16[288,1280]{1,0:T(8,128)(2,1)S(1)} %fusion.19), channel_id=1, source_target_pairs={{0,32},{32,128},{128,160},{160,0},{1,33},{33,129},{129,161},{161,1... | collective-permute-start | bytes 2211848 | tf_op jit(solution)/shard_map/ppermute | solution.py:30
  58.7 2.3 %fusion.18 = f16[288,1280]{1,0:T(8,128)(2,1)S(1)} fusion(f32[288,1280]{1,0:T(8,128)S(1)} %fusion.182, bf16[288,768]{1,0:T(8,128)(2,1)S(1)} %bitcast.107, bf16[768,1280]{1,0:T(8,128)(2,1)} %collective-permute-done.8), kind=kOutput, calls=%fused_computation.32 | convolution fusion | flops 567336960 | bytes 4620288 | tf_op jit(solution)/shard_map/dot_general | solution.py:61
  61.4 0.7 fusion.188
  62.1 14.1 %collective-permute-done.3 = f16[288,1280]{1,0:T(8,128)(2,1)S(1)} collective-permute-done((f16[288,1280]{1,0:T(8,128)(2,1)S(1)}, f16[288,1280]{1,0:T(8,128)(2,1)S(1)}, u32[]{:S(2)}, u32[]{:S(2)}) %collective-permute-start.3) | collective-permute-done | bytes 737312 | tf_op jit(solution)/shard_map/ppermute | solution.py:26
  76.4 2.6 %fusion.17 = f32[288,1280]{1,0:T(8,128)S(1)} fusion(f32[288,1280]{1,0:T(8,128)S(1)} %fusion.196, bf16[288,768]{1,0:T(8,128)(2,1)S(1)} %bitcast.105, bf16[768,1280]{1,0:T(8,128)(2,1)} %collective-permute-done.1, f16[288,1280]{1,0:T(8,128)(2,1)S(1)} %collective-permute-done.4, f16[288,1280]{1,0:T(8,128)(2,1)S(1)} %collective-permute-done.3, ...), kind=kOutput, calls=%fused_computation.31 | convolution fusion | flops 569180160 | bytes 7569408 | tf_op jit(solution)/shard_map/dot_general | solution.py:61
  79.1 2.0 %collective-permute-start.5 = (f16[72,1280]{1,0:T(8,128)(2,1)S(1)}, f16[72,1280]{1,0:T(8,128)(2,1)S(1)}, u32[]{:S(2)}, u32[]{:S(2)}) collective-permute-start(f16[72,1280]{1,0:T(8,128)(2,1)S(1)} %get-tuple-element.30), channel_id=1, source_target_pairs={{0,128},{32,160},{128,0},{160,32},{1,129},{33,161},{129,1},{161,33... | collective-permute-start | bytes 552968 | tf_op jit(solution)/shard_map/ppermute | solution.py:30
  81.7 1.4 collective-permute-start.7
  83.1 7.5 %collective-permute-done.10 = f16[288,1280]{1,0:T(8,128)(2,1)S(1)} collective-permute-done((f16[288,1280]{1,0:T(8,128)(2,1)S(1)}, f16[288,1280]{1,0:T(8,128)(2,1)S(1)}, u32[]{:S(2)}, u32[]{:S(2)}) %collective-permute-start.10) | collective-permute-done | bytes 737312 | tf_op jit(solution)/shard_map/ppermute | solution.py:30
  90.6 2.6 %fusion.16 = f32[288,1280]{1,0:T(8,128)S(1)} fusion(f32[288,1280]{1,0:T(8,128)S(1)} %fusion.188, bf16[288,768]{1,0:T(8,128)(2,1)S(1)} %bitcast.104, bf16[768,1280]{1,0:T(8,128)(2,1)} %collective-permute-done.8, f16[288,1280]{1,0:T(8,128)(2,1)S(1)} %collective-permute-done.11, f16[288,1280]{1,0:T(8,128)(2,1)S(1)} %collective-permute-done.10, ...), kind=kOutput, calls=%fused_computation.30 | convolution fusion | flops 569180160 | bytes 7569408 | tf_op jit(solution)/shard_map/dot_general | solution.py:61
  93.4 0.8 collective-permute-start.13
  94.5 2.2 %collective-permute-start.14 = (f16[72,1280]{1,0:T(8,128)(2,1)S(1)}, f16[72,1280]{1,0:T(8,128)(2,1)S(1)}, u32[]{:S(2)}, u32[]{:S(2)}) collective-permute-start(f16[72,1280]{1,0:T(8,128)(2,1)S(1)} %get-tuple-element.34), channel_id=1, source_target_pairs={{0,3},{1,0},{2,1},{3,2},{4,7},{5,4},{6,5},{7,6},{8,11},{9,8},{10,9... | collective-permute-start | bytes 552968 | tf_op jit(solution)/shard_map/ppermute | solution.py:26
  97.2 5.2 %collective-permute-done.12 = f16[72,1280]{1,0:T(8,128)(2,1)S(1)} collective-permute-done((f16[72,1280]{1,0:T(8,128)(2,1)S(1)}, f16[72,1280]{1,0:T(8,128)(2,1)S(1)}, u32[]{:S(2)}, u32[]{:S(2)}) %collective-permute-start.12) | collective-permute-done | bytes 184352 | tf_op jit(solution)/shard_map/ppermute | solution.py:26
  102.4 2.5 %collective-permute-done.13 = f16[72,1280]{1,0:T(8,128)(2,1)S(1)} collective-permute-done((f16[72,1280]{1,0:T(8,128)(2,1)S(1)}, f16[72,1280]{1,0:T(8,128)(2,1)S(1)}, u32[]{:S(2)}, u32[]{:S(2)}) %collective-permute-start.13) | collective-permute-done | bytes 184352 | tf_op jit(solution)/shard_map/ppermute | solution.py:26
  105.2 1.2 reshape.128
  106.4 8.5 %all-to-all-start = ((f16[8,180,128]{2,1,0:T(8,128)(2,1)}), f16[8,180,128]{2,1,0:T(8,128)(2,1)S(1)}, u32[]{:S(2)}, u32[]{:S(2)}) async-start(f16[8,180,128]{2,1,0:T(8,128)(2,1)} %reshape.128), calls=%async_computation | async-start | bytes 753664 | tf_op jit(solution)/shard_map/all_to_all | solution.py:143
  114.9 14.3 %all-to-all-done = f16[8,180,128]{2,1,0:T(8,128)(2,1)S(1)} async-done(((f16[8,180,128]{2,1,0:T(8,128)(2,1)}), f16[8,180,128]{2,1,0:T(8,128)(2,1)S(1)}, u32[]{:S(2)}, u32[]{:S(2)}) %all-to-all-start) | async-done | bytes 368672 | tf_op jit(solution)/shard_map/all_to_all | solution.py:143
  130.9 25.2 %all_gather.3 = bf16[8,180,128]{2,1,0:T(8,128)(2,1)S(1)} all-gather(bf16[1,180,128]{2,1,0:T(8,128)(2,1)S(1)} %all_gather_reshape.3), channel_id=1, replica_groups=mesh['yh'=2,'core'=2,'yl'=2,'z'=8,'x'=4] {'z'}, dimensions={0}, use_global_device_ids=true | all-gather | bytes 414720 | tf_op jit(solution)/shard_map/all_gather | solution.py:150
  156.5 1.6 collective-permute-start.15
  158.2 6.2 %collective-permute-done.15 = bf16[72,2560]{1,0:T(8,128)(2,1)S(1)} collective-permute-done((bf16[72,2560]{1,0:T(8,128)(2,1)S(1)}, bf16[72,2560]{1,0:T(8,128)(2,1)S(1)}, u32[]{:S(2)}, u32[]{:S(2)}) %collective-permute-start.15) | collective-permute-done | bytes 368672 | tf_op jit(solution)/shard_map/ppermute | solution.py:151
  164.5 1.5 collective-permute-start.17
  166.1 2.1 %collective-permute-start.18 = (bf16[144,2560]{1,0:T(8,128)(2,1)S(1)}, bf16[144,2560]{1,0:T(8,128)(2,1)S(1)}, u32[]{:S(2)}, u32[]{:S(2)}) collective-permute-start(bf16[144,2560]{1,0:T(8,128)(2,1)S(1)} %get-tuple-element.36), channel_id=1, source_target_pairs={{0,3},{1,0},{2,1},{3,2},{4,7},{5,4},{6,5},{7,6},{8,11},{9,8},{10,9... | collective-permute-start | bytes 2211848 | tf_op jit(solution)/shard_map/ppermute | solution.py:26
  168.2 23.5 %collective-permute-done.16 = bf16[144,2560]{1,0:T(8,128)(2,1)S(1)} collective-permute-done((bf16[144,2560]{1,0:T(8,128)(2,1)S(1)}, bf16[144,2560]{1,0:T(8,128)(2,1)S(1)}, u32[]{:S(2)}, u32[]{:S(2)}) %collective-permute-start.16) | collective-permute-done | bytes 737312 | tf_op jit(solution)/shard_map/ppermute | solution.py:26
  192.5 4.4 %convolution_convert_fusion = bf16[384,2560]{1,0:T(8,128)(2,1)} fusion(bf16[576,2560]{1,0:T(8,128)(2,1)S(1)} %constant_dynamic-update-slice_fusion.2, s32[384]{0:T(512)S(1)} %get-tuple-element.57, s32[384]{0:T(512)S(1)} %get-tuple-element.60, s32[384]{0:T(512)S(1)} %get-tuple-element.58, s32[384]{0:T(512)S(1)} %get-tuple-element.61, s32[]{:T(128)S(6)} %axis_index.51, ...), kind=kOutput, calls=%fused_computation | convolution fusion | flops 1143619584 | bytes 4929032 | tf_op jit(solution)/shard_map/dot_general | solution.py:61
  197.0 2.7 %convolution_convert_fusion.1 = bf16[192,2560]{1,0:T(8,128)(2,1)} fusion(bf16[576,2560]{1,0:T(8,128)(2,1)S(1)} %constant_dynamic-update-slice_fusion.2, s32[192]{0:T(256)S(1)} %get-tuple-element.65, s32[192]{0:T(256)S(1)} %get-tuple-element.68, s32[192]{0:T(256)S(1)} %get-tuple-element.66, s32[192]{0:T(256)S(1)} %get-tuple-element.69, s32[]{:T(128)S(6)} %axis_index.51, ...), kind=kOutput, calls=%fused_computation.7 | convolution fusion | flops 571920384 | bytes 3939080 | tf_op jit(solution)/shard_map/dot_general | solution.py:61
  (81 shorter events, 8.6 us)
Async XLA Ops:
  0.6 1.7 copy-start
  2.3 2.4 %copy-start.3 = (bf16[1152,384]{1,0:T(8,128)(2,1)S(1)}, bf16[1152,384]{1,0:T(8,128)(2,1)}, u32[]{:S(2)}) copy-start(bf16[1152,384]{1,0:T(8,128)(2,1)} %constant.285) | copy-start | bytes 2654212
  4.7 3.0 %copy-start.4 = (bf16[96,768]{1,0:T(8,128)(2,1)S(1)}, bf16[96,768]{1,0:T(8,128)(2,1)}, u32[]{:S(2)}) copy-start(bf16[96,768]{1,0:T(8,128)(2,1)} %param.14) | copy-start | bytes 442372
  4.7 2.9 %copy-start.11 = (s32[96]{0:T(128)S(1)}, s32[96]{0:T(128)}, u32[]{:S(2)}) copy-start(s32[96]{0:T(128)} %param.16) | copy-start | bytes 1156
  12.6 14.8 %collective-permute-start = (bf16[1152,768]{0,1:T(8,128)(2,1)}, bf16[1152,768]{0,1:T(8,128)(2,1)}, u32[]{:S(2)}, u32[]{:S(2)}) collective-permute-start(bf16[1152,768]{0,1:T(8,128)(2,1)} %fusion.3), channel_id=1, source_target_pairs={{0,64},{64,0},{1,65},{65,1},{2,66},{66,2},{3,67},{67,3},{4,68},{68... | collective-permute-start | bytes 5308424 | tf_op jit(solution)/shard_map/ppermute | solution.py:34
  16.9 20.8 %collective-permute-start.1 = (bf16[768,1280]{1,0:T(8,128)(2,1)}, bf16[768,1280]{1,0:T(8,128)(2,1)}, u32[]{:S(2)}, u32[]{:S(2)}) collective-permute-start(bf16[768,1280]{1,0:T(8,128)(2,1)} %get-tuple-element.12), channel_id=1, source_target_pairs={{0,64},{64,0},{1,65},{65,1},{2,66},{66,2},{3,67},{67,3},{4,68},{68... | collective-permute-start | bytes 5898248 | tf_op jit(solution)/shard_map/ppermute | solution.py:34
  17.4 33.8 %collective-permute-start.8 = (bf16[768,1280]{1,0:T(8,128)(2,1)}, bf16[768,1280]{1,0:T(8,128)(2,1)}, u32[]{:S(2)}, u32[]{:S(2)}) collective-permute-start(bf16[768,1280]{1,0:T(8,128)(2,1)} %get-tuple-element.13), channel_id=1, source_target_pairs={{0,64},{64,0},{1,65},{65,1},{2,66},{66,2},{3,67},{67,3},{4,68},{68... | collective-permute-start | bytes 5898248 | tf_op jit(solution)/shard_map/ppermute | solution.py:34
  30.0 2.1 %copy-start.2 = (bf16[768,2560]{1,0:T(8,128)(2,1)S(1)}, bf16[768,2560]{1,0:T(8,128)(2,1)}, u32[]{:S(2)}) copy-start(bf16[768,2560]{1,0:T(8,128)(2,1)} %param.15) | copy-start | bytes 11796484
  40.0 21.0 %collective-permute-start.2 = (f16[288,1280]{1,0:T(8,128)(2,1)S(1)}, f16[288,1280]{1,0:T(8,128)(2,1)S(1)}, u32[]{:S(2)}, u32[]{:S(2)}) collective-permute-start(f16[288,1280]{1,0:T(8,128)(2,1)S(1)} %fusion.23), channel_id=1, source_target_pairs={{0,2},{1,3},{2,0},{3,1},{4,6},{5,7},{6,4},{7,5},{8,10},{9,11},{10,... | collective-permute-start | bytes 2211848 | tf_op jit(solution)/shard_map/ppermute | solution.py:26
  45.4 30.8 %collective-permute-start.3 = (f16[288,1280]{1,0:T(8,128)(2,1)S(1)}, f16[288,1280]{1,0:T(8,128)(2,1)S(1)}, u32[]{:S(2)}, u32[]{:S(2)}) collective-permute-start(f16[288,1280]{1,0:T(8,128)(2,1)S(1)} %fusion.22), channel_id=1, source_target_pairs={{0,1},{1,2},{2,3},{3,0},{4,5},{5,6},{6,7},{7,4},{8,9},{9,10},{10,1... | collective-permute-start | bytes 2211848 | tf_op jit(solution)/shard_map/ppermute | solution.py:26
  48.4 28.0 %collective-permute-start.4 = (f16[288,1280]{1,0:T(8,128)(2,1)S(1)}, f16[288,1280]{1,0:T(8,128)(2,1)S(1)}, u32[]{:S(2)}, u32[]{:S(2)}) collective-permute-start(f16[288,1280]{1,0:T(8,128)(2,1)S(1)} %fusion.21), channel_id=1, source_target_pairs={{0,3},{1,0},{2,1},{3,2},{4,7},{5,4},{6,5},{7,6},{8,11},{9,8},{10,9... | collective-permute-start | bytes 2211848 | tf_op jit(solution)/shard_map/ppermute | solution.py:26
  53.5 28.2 %collective-permute-start.9 = (f16[288,1280]{1,0:T(8,128)(2,1)S(1)}, f16[288,1280]{1,0:T(8,128)(2,1)S(1)}, u32[]{:S(2)}, u32[]{:S(2)}) collective-permute-start(f16[288,1280]{1,0:T(8,128)(2,1)S(1)} %fusion.20), channel_id=1, source_target_pairs={{0,128},{32,160},{128,0},{160,32},{1,129},{33,161},{129,1},{161,33... | collective-permute-start | bytes 2211848 | tf_op jit(solution)/shard_map/ppermute | solution.py:30
  56.4 34.2 %collective-permute-start.10 = (f16[288,1280]{1,0:T(8,128)(2,1)S(1)}, f16[288,1280]{1,0:T(8,128)(2,1)S(1)}, u32[]{:S(2)}, u32[]{:S(2)}) collective-permute-start(f16[288,1280]{1,0:T(8,128)(2,1)S(1)} %fusion.19), channel_id=1, source_target_pairs={{0,32},{32,128},{128,160},{160,0},{1,33},{33,129},{129,161},{161,1... | collective-permute-start | bytes 2211848 | tf_op jit(solution)/shard_map/ppermute | solution.py:30
  61.1 29.5 %collective-permute-start.11 = (f16[288,1280]{1,0:T(8,128)(2,1)S(1)}, f16[288,1280]{1,0:T(8,128)(2,1)S(1)}, u32[]{:S(2)}, u32[]{:S(2)}) collective-permute-start(f16[288,1280]{1,0:T(8,128)(2,1)S(1)} %fusion.18), channel_id=1, source_target_pairs={{0,160},{32,0},{128,32},{160,128},{1,161},{33,1},{129,33},{161,129... | collective-permute-start | bytes 2211848 | tf_op jit(solution)/shard_map/ppermute | solution.py:30
  79.1 15.5 %collective-permute-start.5 = (f16[72,1280]{1,0:T(8,128)(2,1)S(1)}, f16[72,1280]{1,0:T(8,128)(2,1)S(1)}, u32[]{:S(2)}, u32[]{:S(2)}) collective-permute-start(f16[72,1280]{1,0:T(8,128)(2,1)S(1)} %get-tuple-element.30), channel_id=1, source_target_pairs={{0,128},{32,160},{128,0},{160,32},{1,129},{33,161},{129,1},{161,33... | collective-permute-start | bytes 552968 | tf_op jit(solution)/shard_map/ppermute | solution.py:30
  81.1 15.9 %collective-permute-start.6 = (f16[72,1280]{1,0:T(8,128)(2,1)S(1)}, f16[72,1280]{1,0:T(8,128)(2,1)S(1)}, u32[]{:S(2)}, u32[]{:S(2)}) collective-permute-start(f16[72,1280]{1,0:T(8,128)(2,1)S(1)} %get-tuple-element.32), channel_id=1, source_target_pairs={{0,32},{32,128},{128,160},{160,0},{1,33},{33,129},{129,161},{161,1... | collective-permute-start | bytes 552968 | tf_op jit(solution)/shard_map/ppermute | solution.py:30
  81.7 15.4 %collective-permute-start.7 = (f16[72,1280]{1,0:T(8,128)(2,1)S(1)}, f16[72,1280]{1,0:T(8,128)(2,1)S(1)}, u32[]{:S(2)}, u32[]{:S(2)}) collective-permute-start(f16[72,1280]{1,0:T(8,128)(2,1)S(1)} %get-tuple-element.31), channel_id=1, source_target_pairs={{0,160},{32,0},{128,32},{160,128},{1,161},{33,1},{129,33},{161,129... | collective-permute-start | bytes 552968 | tf_op jit(solution)/shard_map/ppermute | solution.py:30
  93.3 9.1 %collective-permute-start.12 = (f16[72,1280]{1,0:T(8,128)(2,1)S(1)}, f16[72,1280]{1,0:T(8,128)(2,1)S(1)}, u32[]{:S(2)}, u32[]{:S(2)}) collective-permute-start(f16[72,1280]{1,0:T(8,128)(2,1)S(1)} %get-tuple-element.33), channel_id=1, source_target_pairs={{0,2},{1,3},{2,0},{3,1},{4,6},{5,7},{6,4},{7,5},{8,10},{9,11},{10,... | collective-permute-start | bytes 552968 | tf_op jit(solution)/shard_map/ppermute | solution.py:26
  93.4 11.6 %collective-permute-start.13 = (f16[72,1280]{1,0:T(8,128)(2,1)S(1)}, f16[72,1280]{1,0:T(8,128)(2,1)S(1)}, u32[]{:S(2)}, u32[]{:S(2)}) collective-permute-start(f16[72,1280]{1,0:T(8,128)(2,1)S(1)} %get-tuple-element.35), channel_id=1, source_target_pairs={{0,1},{1,2},{2,3},{3,0},{4,5},{5,6},{6,7},{7,4},{8,9},{9,10},{10,1... | collective-permute-start | bytes 552968 | tf_op jit(solution)/shard_map/ppermute | solution.py:26
  94.5 10.4 %collective-permute-start.14 = (f16[72,1280]{1,0:T(8,128)(2,1)S(1)}, f16[72,1280]{1,0:T(8,128)(2,1)S(1)}, u32[]{:S(2)}, u32[]{:S(2)}) collective-permute-start(f16[72,1280]{1,0:T(8,128)(2,1)S(1)} %get-tuple-element.34), channel_id=1, source_target_pairs={{0,3},{1,0},{2,1},{3,2},{4,7},{5,4},{6,5},{7,6},{8,11},{9,8},{10,9... | collective-permute-start | bytes 552968 | tf_op jit(solution)/shard_map/ppermute | solution.py:26
  97.1 32.2 %copy-start.5 = (f32[6,2560]{1,0:T(8,128)S(1)}, f32[6,2560]{1,0:T(8,128)}, u32[]{:S(2)}) copy-start(f32[6,2560]{1,0:T(8,128)} %param.18) | copy-start | bytes 184324
  97.2 32.2 %copy-start.6 = (f32[6,2560]{1,0:T(8,128)S(1)}, f32[6,2560]{1,0:T(8,128)}, u32[]{:S(2)}) copy-start(f32[6,2560]{1,0:T(8,128)} %param.20) | copy-start | bytes 184324
  97.2 32.2 %copy-start.7 = (f32[6,2560]{1,0:T(8,128)S(1)}, f32[6,2560]{1,0:T(8,128)}, u32[]{:S(2)}) copy-start(f32[6,2560]{1,0:T(8,128)} %param.19) | copy-start | bytes 184324
  105.1 25.0 %copy-start.8 = (f32[3,2560]{1,0:T(4,128)S(1)}, f32[3,2560]{1,0:T(4,128)}, u32[]{:S(2)}) copy-start(f32[3,2560]{1,0:T(4,128)} %param.21) | copy-start | bytes 92164
  105.1 25.0 %copy-start.9 = (f32[3,2560]{1,0:T(4,128)S(1)}, f32[3,2560]{1,0:T(4,128)}, u32[]{:S(2)}) copy-start(f32[3,2560]{1,0:T(4,128)} %param.23) | copy-start | bytes 92164
  105.1 25.0 %copy-start.10 = (f32[3,2560]{1,0:T(4,128)S(1)}, f32[3,2560]{1,0:T(4,128)}, u32[]{:S(2)}) copy-start(f32[3,2560]{1,0:T(4,128)} %param.22) | copy-start | bytes 92164
  106.4 22.8 %all-to-all-start = ((f16[8,180,128]{2,1,0:T(8,128)(2,1)}), f16[8,180,128]{2,1,0:T(8,128)(2,1)S(1)}, u32[]{:S(2)}, u32[]{:S(2)}) async-start(f16[8,180,128]{2,1,0:T(8,128)(2,1)} %reshape.128), calls=%async_computation | async-start | bytes 753664 | tf_op jit(solution)/shard_map/all_to_all | solution.py:143
  156.5 7.9 %collective-permute-start.15 = (bf16[72,2560]{1,0:T(8,128)(2,1)S(1)}, bf16[72,2560]{1,0:T(8,128)(2,1)S(1)}, u32[]{:S(2)}, u32[]{:S(2)}) collective-permute-start(bf16[72,2560]{1,0:T(8,128)(2,1)S(1)} %reshape.129), channel_id=1, source_target_pairs={{0,32},{32,0},{1,33},{33,1},{2,34},{34,2},{3,35},{35,3},{4,36},{36... | collective-permute-start | bytes 1105928 | tf_op jit(solution)/shard_map/ppermute | solution.py:151
  164.4 27.3 %collective-permute-start.16 = (bf16[144,2560]{1,0:T(8,128)(2,1)S(1)}, bf16[144,2560]{1,0:T(8,128)(2,1)S(1)}, u32[]{:S(2)}, u32[]{:S(2)}) collective-permute-start(bf16[144,2560]{1,0:T(8,128)(2,1)S(1)} %get-tuple-element.36), channel_id=1, source_target_pairs={{0,1},{1,2},{2,3},{3,0},{4,5},{5,6},{6,7},{7,4},{8,9},{9,10},{10,1... | collective-permute-start | bytes 2211848 | tf_op jit(solution)/shard_map/ppermute | solution.py:26
  164.5 27.2 %collective-permute-start.17 = (bf16[144,2560]{1,0:T(8,128)(2,1)S(1)}, bf16[144,2560]{1,0:T(8,128)(2,1)S(1)}, u32[]{:S(2)}, u32[]{:S(2)}) collective-permute-start(bf16[144,2560]{1,0:T(8,128)(2,1)S(1)} %get-tuple-element.36), channel_id=1, source_target_pairs={{0,2},{1,3},{2,0},{3,1},{4,6},{5,7},{6,4},{7,5},{8,10},{9,11},{10,... | collective-permute-start | bytes 2211848 | tf_op jit(solution)/shard_map/ppermute | solution.py:26
  166.1 26.4 %collective-permute-start.18 = (bf16[144,2560]{1,0:T(8,128)(2,1)S(1)}, bf16[144,2560]{1,0:T(8,128)(2,1)S(1)}, u32[]{:S(2)}, u32[]{:S(2)}) collective-permute-start(bf16[144,2560]{1,0:T(8,128)(2,1)S(1)} %get-tuple-element.36), channel_id=1, source_target_pairs={{0,3},{1,0},{2,1},{3,2},{4,7},{5,4},{6,5},{7,6},{8,11},{9,8},{10,9... | collective-permute-start | bytes 2211848 | tf_op jit(solution)/shard_map/ppermute | solution.py:26
  197.0 2.7 %copy-start.1 = (bf16[768,1536]{1,0:T(8,128)(2,1)S(1)}, bf16[768,1536]{1,0:T(8,128)(2,1)}, u32[]{:S(2)}) copy-start(bf16[768,1536]{1,0:T(8,128)(2,1)} %param.13) | copy-start | bytes 7077892

commit v2 on v1

v2 whole, which is shorter than its diff:
```python
import jax
import jax.numpy as jnp
import numpy as np
from jax import lax
from jax.experimental import pallas as pl
from jax.experimental.pallas import tpu as pltpu
from jax.sharding import Mesh, PartitionSpec as P

AXES = ("yh", "core", "yl", "z", "x")
NX, NY, NZ = 4, 4, 8
SCALE = 0.25
BF = jnp.bfloat16
F32 = jnp.float32
F16 = jnp.float16


def adamw(grad, master, moment, second):
    corr_one = 1.0 - 0.9**20
    corr_two = 1.0 - 0.95**20
    new_moment = 0.9 * moment + 0.1 * grad
    new_second = 0.95 * second + 0.05 * grad * grad
    step_dir = new_moment / corr_one / (jnp.sqrt(new_second / corr_two) + 1e-08)
    new_master = master - 0.02 * (step_dir + 0.1 * master)
    return (new_moment, new_second, new_master.astype(BF))


def x_ring(v, d):
    return lax.ppermute(v, "x", [(i, (i + d) % NX) for i in range(NX)])


def y_ring(v, d):
    return lax.ppermute(v, ("yh", "yl"), [(i, (i + d) % NY) for i in range(NY)])


def y_swap(v):
    return lax.ppermute(v, "yl", [(0, 1), (1, 0)])


def core_swap(v):
    return lax.ppermute(v, "core", [(0, 1), (1, 0)])


def row_order(sr, rr):
    rows = sr + rr
    n = NX * 2 * NZ * rows
    xs, ys, zs, i = np.meshgrid(np.arange(NX), np.arange(2), np.arange(NZ), np.arange(rows), indexing="ij")
    dev = (ys * NZ + zs) * NX + xs
    flat = np.arange(n)
    keep = (i < sr).reshape(-1)
    shared = np.zeros((n, 2 * NZ * NX * sr), np.float32)
    shared[flat[keep], (dev * sr + i).reshape(-1)[keep]] = 1
    routed = np.zeros((2, n, 2, 2 * NZ * NX * rr), np.float32)
    for core in range(2):
        routed[core, flat[~keep], core, (dev * rr + i - sr).reshape(-1)[~keep]] = 1
    return shared.astype(BF), routed.reshape(2, n, -1).astype(BF)


def dot_t(a, b):
    return lax.dot_general(a, b, (((1,), (1,)), ((), ())), preferred_element_type=F32)


def dot(a, b):
    return jnp.dot(a, b, preferred_element_type=F32)


def order_kernel(core_ref, shared_ref, routed_ref, shared_order_ref, routed_order_ref, place_ref, out_ref):
    slots = dot_t(routed_order_ref[0], routed_ref[...]).astype(BF)
    total = dot_t(shared_order_ref[...], shared_ref[...]) + dot(slots, place_ref[...])
    out_ref[...] = total.astype(BF).reshape(out_ref.shape)


def ordered(core, hid_shared, hid_routed, shared_order, routed_order, place):
    tok = hid_shared.shape[0]
    slots = hid_routed.shape[0]
    n, cut = shared_order.shape
    pair = routed_order.shape[2]
    return pl.pallas_call(
        order_kernel,
        grid_spec=pltpu.PrefetchScalarGridSpec(
            num_scalar_prefetch=1,
            grid=(2,),
            in_specs=[
                pl.BlockSpec((tok, cut), lambda h, c: (0, h * 2 + c[0])),
                pl.BlockSpec((slots, pair), lambda h, c: (0, h)),
                pl.BlockSpec((n, cut), lambda h, c: (0, 0)),
                pl.BlockSpec((1, n, pair), lambda h, c: (c[0], 0, 0)),
                pl.BlockSpec((slots, tok), lambda h, c: (0, 0)),
            ],
            out_specs=pl.BlockSpec((NX, 1, n // NX, tok), lambda h, c: (0, h, 0, 0)),
        ),
        out_shape=jax.ShapeDtypeStruct((NX, 2, n // NX, tok), BF),
        compiler_params=pltpu.CompilerParams(vmem_limit_bytes=32 * 2**20),
        cost_estimate=pl.CostEstimate(flops=4 * n * cut * tok, bytes_accessed=6 * n * tok, transcendentals=0),
    )(core.reshape(1), hid_shared, hid_routed, shared_order, routed_order, place)


def local(
    hid_shared,
    hid_routed,
    out_grad,
    slot_token,
    slot_count,
    master_shared,
    moment_shared,
    second_shared,
    master_routed,
    moment_routed,
    second_routed,
):
    tok, width = out_grad.shape
    slots = hid_routed.shape[0]
    sr, rr = master_shared.shape[0], master_routed.shape[0]
    rows = sr + rr
    half = width // 2
    group = NZ * rows
    core = lax.axis_index("core")
    x = lax.axis_index("x")
    yh, yl = lax.axis_index("yh"), lax.axis_index("yl")
    y = yh * 2 + yl

    shared_order, routed_order = (jnp.asarray(v) for v in row_order(sr, rr))
    live = lax.iota(jnp.int32, slots) < slot_count[0]
    place = (slot_token[:, None] == lax.broadcasted_iota(jnp.int32, (slots, tok), 1)) & live[:, None]
    place = place.astype(BF)

    def activ(k):
        return ordered(k, hid_shared, hid_routed, shared_order, routed_order, place)

    out_far = core_swap(out_grad)
    act_far = core_swap(activ(1 - core)).reshape(NX, NY, group, tok)
    act_near = activ(core).reshape(NX, NY, group, tok)

    def term(near, far, part, index):
        def pick(a):
            return lax.dynamic_index_in_dim(a, index, part, keepdims=False).reshape(-1, tok)

        cols = slice(part * half, (part + 1) * half)
        total = dot(pick(near), out_grad[:, cols]) + dot(pick(far), out_far[:, cols])
        return SCALE * total

    rings = (x_ring, y_ring)
    place_of = (x, y)
    got = ([], [])
    far = act_far
    for d in (2, 1, 3):
        for part in range(2):
            sent = term(act_near, far, part, (place_of[part] + d) % 4).astype(F16)
            got[part].append(rings[part](sent, d))
    firsts = []
    for part in range(2):
        total = term(act_near, far, part, place_of[part])
        for g in got[part]:
            total = total + g.astype(F32)
        firsts.append(total.reshape(4, group, half))
    seconds = []
    for part in range(2):
        ring, me = rings[1 - part], place_of[1 - part]

        def pick(index):
            return lax.dynamic_index_in_dim(firsts[part], index, 0, keepdims=False)

        back = [ring(pick((me + d) % 4).astype(F16), d) for d in (2, 1, 3)]
        total = pick(me)
        for g in back:
            total = total + g.astype(F32)
        seconds.append(total.astype(F16))
    last = jnp.concatenate(seconds, axis=1).reshape(NZ, rows * width // 128, 128)
    last = lax.all_to_all(last, "z", 0, 0)
    grad = (last.astype(F32).sum(axis=0) * (1.0 / SCALE)).reshape(rows, width)

    moment_s, second_s, weight_s = adamw(grad[:sr], master_shared, moment_shared, second_shared)
    moment_r, second_r, weight_r = adamw(grad[sr:], master_routed, moment_routed, second_routed)

    weight_s = weight_s.reshape(1, sr * width // 128, 128)
    s_all = lax.all_to_all(jnp.broadcast_to(weight_s, (NZ,) + weight_s.shape[1:]), "z", 0, 0)
    weight_r = weight_r.reshape(rr * width // 128, 128)
    r_all = jnp.concatenate([weight_r] + [x_ring(weight_r, d) for d in (1, 2, 3)], axis=0)
    s_all = s_all.reshape(NZ * sr, width)
    s_all = jnp.concatenate([s_all, y_swap(s_all)], axis=0)
    r_all = jnp.concatenate([r_all, y_swap(r_all)], axis=0).reshape(2 * NX * rr, width)
    s_all = jnp.concatenate([s_all] + [x_ring(s_all, d) for d in (1, 2, 3)], axis=0)
    r_all = lax.all_gather(r_all, "z", axis=0, tiled=True)

    def final(full, count, index):
        n = full.shape[0]
        r = lax.iota(jnp.int32, n)
        i = r % count
        back = (x - (r // count) % NX) % NX
        zz = (r // (count * NX)) % NZ
        flip = (r // (count * NX * NZ)) ^ yl
        want = lax.optimization_barrier(index(back, flip, zz) * count + i)
        take = want[:, None] == lax.broadcasted_iota(jnp.int32, (n, n), 1)
        return dot(take.astype(BF), full).astype(BF)

    shared = final(s_all, sr, lambda back, flip, zz: (back * 2 + flip) * NZ + zz)
    routed = final(r_all, rr, lambda back, flip, zz: (zz * 2 + flip) * NX + back)
    return (moment_s, second_s, moment_r, second_r, shared, routed)


def solution(mesh):
    fine = Mesh(mesh.devices.reshape(2, 2, 2, NZ, NX), AXES)
    split = P(AXES, None)
    flat = P(AXES)
    cuts = P(("yh", "core"), None)
    return jax.shard_map(
        local,
        mesh=fine,
        in_specs=(split, split, split, flat, flat) + (split,) * 6,
        out_specs=(split,) * 4 + (cuts,) * 2,
        check_vma=False,
    )
```

time: 200 us -> 186 us (0.930)
  blocking collectives: 25.2 us -> 50.8 us
  waiting for transfers between devices: 74.8 us -> 50.7 us
  matrix products: 51.2 us -> 28.9 us
  Pallas kernels: 0 us -> 6.25 us
    all_to_all x0 -> x1, blocking collectives: none -> 22.6 us  [local(): last = lax.all_to_all(last, 'z', 0, 0)]
    all_to_all x1, waiting for transfers between devices: 14.3 us -> 0.01 us  [local(): lax.all_to_all(jnp.broadcast_to(weight_s, (NZ,) + weight_s.shape[1:]), 'z...]
    dot_general x20 -> x18, matrix products: 40.7 us -> 28.9 us  [dot(): return jnp.dot(a, b, preferred_element_type=F32)]
    ppermute x9 -> x12, waiting for transfers between devices: 46.2 us -> 34.6 us  [x_ring(): return lax.ppermute(v, 'x', [(i, (i + d) % NX) for i in range(NX)])]
    dot_general x4 -> x0, matrix products: 10.6 us -> none  [dot_t(): lax.dot_general(a, b, (((1,), (1,)), ((), ())), preferred_element_type=F32)]
    pallas_call x0 -> x2, Pallas kernels: none -> 6.25 us  [ordered(): pl.pallas_call(order_kernel, grid_spec=pltpu.PrefetchScalarGridSpec(num_s...]
    all_to_all x1, starting transfers between devices: 8.47 us -> 3.41 us  [local(): lax.all_to_all(jnp.broadcast_to(weight_s, (NZ,) + weight_s.shape[1:]), 'z...]
    ppermute x9 -> x12, starting transfers between devices: 13.3 us -> 18.3 us  [x_ring(): return lax.ppermute(v, 'x', [(i, (i + d) % NX) for i in range(NX)])]
  transfers between devices with their start and end apart: 20 -> 23, of which waited for: 11 -> 13; matrix products, arithmetic and copies ran while one was open for 21% -> 16% of each run, Pallas kernels for 0% -> 1%
where the time goes in v2:
time: 186 us
  blocking collectives  50.8 us (27%)
  waiting for transfers between devices  50.7 us (27%)
  starting transfers between devices  32.1 us (17%)
  matrix products  28.9 us (16%)
  local copies, waits for them, and re-layouts  12.4 us (7%)
  Pallas kernels  6.25 us (3%)
  other arithmetic  2.83 us (2%)
    ppermute x12, waiting for transfers between devices, x_ring(): return lax.ppermute(v, 'x', [(i, (i + d) % NX) for i in range(NX)])  34.6 us
    dot_general x18, matrix products, dot(): return jnp.dot(a, b, preferred_element_type=F32)  28.9 us
    all_gather x1, blocking collectives, local(): r_all = lax.all_gather(r_all, 'z', axis=0, tiled=True)  28.3 us
    all_to_all x1, blocking collectives, local(): last = lax.all_to_all(last, 'z', 0, 0)  22.6 us
    ppermute x12, starting transfers between devices, x_ring(): return lax.ppermute(v, 'x', [(i, (i + d) % NX) for i in range(NX)])  18.3 us
    ppermute x6, waiting for transfers between devices, y_ring(): return lax.ppermute(v, ('yh', 'yl'), [(i, (i + d) % NY) for i in range(NY)])  8.17 us
    ppermute x2, waiting for transfers between devices, y_swap(): return lax.ppermute(v, 'yl', [(0, 1), (1, 0)])  7.91 us
    ppermute x6, starting transfers between devices, y_ring(): return lax.ppermute(v, ('yh', 'yl'), [(i, (i + d) % NY) for i in range(NY)])  7.18 us
  transfers between devices with their start and end apart: 23, of which 13 were waited for; matrix products, arithmetic and copies ran while one was open for 16% of the time, Pallas kernels for 1%

profile of v2, /device:TPU:16, one launch (start us, length us, event | category | flops | bytes accessed | tf_op | source)
XLA Modules:
  0.0 185.7 jit_solution(10662081136529194731)
XLA Ops:
  1.3 0.8 fusion.52.place_ref
  2.1 1.7 copy-done
  3.7 1.2 copy-done.2
  4.9 1.0 copy-done.4
  5.9 0.9 copy-done.6
  6.8 3.5 %shard_map.173 = bf16[4,2,144,768]{3,2,1,0:T(8,128)(2,1)} custom-call(s32[1]{0:T(128)} %bitcast.4.core_ref, bf16[768,1536]{1,0:T(8,128)(2,1)S(1)} %copy-done, bf16[96,768]{1,0:T(8,128)(2,1)S(1)} %copy-done.6, bf16[576,384]{1,0:T(8,128)(2,1)S(1)} %copy-done.4, bf16[2,576,384]{2,1,0:T(8,128)(2,1)S(1)} %copy-done.2, bf16[96,768]{1,0:T(8,128)(2,1)S(1)} %fusion.52.place_ref), custom_call_target="tpu_custom_call" | custom-call | flops 679477248 | bytes 2654208 | tf_op jit(solution)/shard_map/pallas_call | solution.py:77
  10.9 1.0 copy-done.5
  11.9 2.7 %shard_map.172 = bf16[4,2,144,768]{3,2,1,0:T(8,128)(2,1)S(1)} custom-call(s32[1]{0:T(128)} %bitcast.core_ref, bf16[768,1536]{1,0:T(8,128)(2,1)S(1)} %copy-done.1, bf16[96,768]{1,0:T(8,128)(2,1)S(1)} %copy-done.7, bf16[576,384]{1,0:T(8,128)(2,1)S(1)} %copy-done.5, bf16[2,576,384]{2,1,0:T(8,128)(2,1)S(1)} %copy-done.3, bf16[96,768]{1,0:T(8,128)(2,1)S(1)} %fusion.52.place_ref), custom_call_target="tpu_custom_call" | custom-call | flops 679477248 | bytes 2654208 | tf_op jit(solution)/shard_map/pallas_call | solution.py:77
  14.6 1.7 constant_dynamic-slice_fusion.12
  16.3 1.9 %constant_dynamic-slice_fusion.4 = (bf16[4,1,72,768]{3,2,1,0:T(8,128)(2,1)S(1)}, bf16[4,1,72,768]{3,2,1,0:T(8,128)(2,1)S(1)}, bf16[4,1,72,768]{3,2,1,0:T(8,128)(...) fusion(bf16[4,4,72,768]{3,2,1,0:T(8,128)(2,1)} %bitcast.5, ...), kind=kLoop, calls=%fused_computation.104 | loop fusion | bytes 7077904 | tf_op jit(solution)/shard_map/jit(dynamic_index_in_dim)/dynamic_slice | solution.py:135
  18.2 0.8 copy-done.14
  20.5 0.7 fusion.36
  21.2 0.7 fusion.42
  24.2 2.3 %fusion.19 = f16[288,1280]{1,0:T(8,128)(2,1)S(1)} fusion(f32[288,1280]{1,0:T(8,128)S(1)} %fusion.40, bf16[288,768]{1,0:T(8,128)(2,1)S(1)} %bitcast.84, bf16[768,2560]{1,0:T(8,128)(2,1)} %collective-permute-done.1), kind=kOutput, calls=%fused_computation.29 | convolution fusion | flops 567336960 | bytes 4620288 | tf_op jit(solution)/shard_map/dot_general | solution.py:63
  26.6 3.1 %collective-permute-start.2 = (f16[288,1280]{1,0:T(8,128)(2,1)S(1)}, f16[288,1280]{1,0:T(8,128)(2,1)S(1)}, u32[]{:S(2)}, u32[]{:S(2)}) collective-permute-start(f16[288,1280]{1,0:T(8,128)(2,1)S(1)} %fusion.19), channel_id=1, source_target_pairs={{0,2},{1,3},{2,0},{3,1},{4,6},{5,7},{6,4},{7,5},{8,10},{9,11},{10,... | collective-permute-start | bytes 2211848 | tf_op jit(solution)/shard_map/ppermute | solution.py:28
  29.7 2.3 %fusion.18 = f16[288,1280]{1,0:T(8,128)(2,1)S(1)} fusion(f32[288,1280]{1,0:T(8,128)S(1)} %fusion.38, bf16[288,768]{1,0:T(8,128)(2,1)S(1)} %bitcast.83, bf16[768,2560]{1,0:T(8,128)(2,1)} %collective-permute-done.1), kind=kOutput, calls=%fused_computation.28 | convolution fusion | flops 567336960 | bytes 4620288 | tf_op jit(solution)/shard_map/dot_general | solution.py:63
  32.7 2.3 %fusion.17 = f16[288,1280]{1,0:T(8,128)(2,1)S(1)} fusion(f32[288,1280]{1,0:T(8,128)S(1)} %fusion.36, bf16[288,768]{1,0:T(8,128)(2,1)S(1)} %bitcast.82, bf16[768,2560]{1,0:T(8,128)(2,1)} %collective-permute-done.1), kind=kOutput, calls=%fused_computation.27 | convolution fusion | flops 567336960 | bytes 4620288 | tf_op jit(solution)/shard_map/dot_general | solution.py:63
  35.0 2.9 %collective-permute-start.4 = (f16[288,1280]{1,0:T(8,128)(2,1)S(1)}, f16[288,1280]{1,0:T(8,128)(2,1)S(1)}, u32[]{:S(2)}, u32[]{:S(2)}) collective-permute-start(f16[288,1280]{1,0:T(8,128)(2,1)S(1)} %fusion.17), channel_id=1, source_target_pairs={{0,3},{1,0},{2,1},{3,2},{4,7},{5,4},{6,5},{7,6},{8,11},{9,8},{10,9... | collective-permute-start | bytes 2211848 | tf_op jit(solution)/shard_map/ppermute | solution.py:28
  37.9 2.3 %fusion.16 = f16[288,1280]{1,0:T(8,128)(2,1)S(1)} fusion(f32[288,1280]{1,0:T(8,128)S(1)} %fusion.32, bf16[288,768]{1,0:T(8,128)(2,1)S(1)} %bitcast.81, bf16[768,2560]{1,0:T(8,128)(2,1)} %collective-permute-done.1), kind=kOutput, calls=%fused_computation.26 | convolution fusion | flops 567336960 | bytes 4620288 | tf_op jit(solution)/shard_map/dot_general | solution.py:63
  40.6 2.3 %fusion.15 = f16[288,1280]{1,0:T(8,128)(2,1)S(1)} fusion(f32[288,1280]{1,0:T(8,128)S(1)} %fusion.30, bf16[288,768]{1,0:T(8,128)(2,1)S(1)} %bitcast.80, bf16[768,2560]{1,0:T(8,128)(2,1)} %collective-permute-done.1), kind=kOutput, calls=%fused_computation.25 | convolution fusion | flops 567336960 | bytes 4620288 | tf_op jit(solution)/shard_map/dot_general | solution.py:63
  43.0 2.3 %collective-permute-start.9 = (f16[288,1280]{1,0:T(8,128)(2,1)S(1)}, f16[288,1280]{1,0:T(8,128)(2,1)S(1)}, u32[]{:S(2)}, u32[]{:S(2)}) collective-permute-start(f16[288,1280]{1,0:T(8,128)(2,1)S(1)} %fusion.15), channel_id=1, source_target_pairs={{0,32},{32,128},{128,160},{160,0},{1,33},{33,129},{129,161},{161,1... | collective-permute-start | bytes 2211848 | tf_op jit(solution)/shard_map/ppermute | solution.py:32
  45.2 2.3 %fusion.14 = f16[288,1280]{1,0:T(8,128)(2,1)S(1)} fusion(f32[288,1280]{1,0:T(8,128)S(1)} %fusion.28, bf16[288,768]{1,0:T(8,128)(2,1)S(1)} %bitcast.79, bf16[768,2560]{1,0:T(8,128)(2,1)} %collective-permute-done.1), kind=kOutput, calls=%fused_computation.24 | convolution fusion | flops 567336960 | bytes 4620288 | tf_op jit(solution)/shard_map/dot_general | solution.py:63
  48.7 13.6 %collective-permute-done.3 = f16[288,1280]{1,0:T(8,128)(2,1)S(1)} collective-permute-done((f16[288,1280]{1,0:T(8,128)(2,1)S(1)}, f16[288,1280]{1,0:T(8,128)(2,1)S(1)}, u32[]{:S(2)}, u32[]{:S(2)}) %collective-permute-start.3) | collective-permute-done | bytes 737312 | tf_op jit(solution)/shard_map/ppermute | solution.py:28
  62.5 2.6 %fusion.13 = f32[288,1280]{1,0:T(8,128)S(1)} fusion(f32[288,1280]{1,0:T(8,128)S(1)} %fusion.42, bf16[288,768]{1,0:T(8,128)(2,1)S(1)} %bitcast.77, f16[288,1280]{1,0:T(8,128)(2,1)S(1)} %collective-permute-done.4, f16[288,1280]{1,0:T(8,128)(2,1)S(1)} %collective-permute-done.3, f16[288,1280]{1,0:T(8,128)(2,1)S(1)} %collective-permute-done.2, ...), kind=kOutput, calls=%fused_computation.23 | convolution fusion | flops 569180160 | bytes 7569408 | tf_op jit(solution)/shard_map/dot_general | solution.py:63
  65.1 2.0 %collective-permute-start.5 = (f16[72,1280]{1,0:T(8,128)(2,1)S(1)}, f16[72,1280]{1,0:T(8,128)(2,1)S(1)}, u32[]{:S(2)}, u32[]{:S(2)}) collective-permute-start(f16[72,1280]{1,0:T(8,128)(2,1)S(1)} %get-tuple-element.28), channel_id=1, source_target_pairs={{0,128},{32,160},{128,0},{160,32},{1,129},{33,161},{129,1},{161,33... | collective-permute-start | bytes 552968 | tf_op jit(solution)/shard_map/ppermute | solution.py:32
  67.8 1.5 collective-permute-start.7
  69.2 7.9 %collective-permute-done.9 = f16[288,1280]{1,0:T(8,128)(2,1)S(1)} collective-permute-done((f16[288,1280]{1,0:T(8,128)(2,1)S(1)}, f16[288,1280]{1,0:T(8,128)(2,1)S(1)}, u32[]{:S(2)}, u32[]{:S(2)}) %collective-permute-start.9) | collective-permute-done | bytes 737312 | tf_op jit(solution)/shard_map/ppermute | solution.py:32
  77.1 2.6 %fusion.12 = f32[288,1280]{1,0:T(8,128)S(1)} fusion(f32[288,1280]{1,0:T(8,128)S(1)} %fusion.34, bf16[288,768]{1,0:T(8,128)(2,1)S(1)} %bitcast.76, f16[288,1280]{1,0:T(8,128)(2,1)S(1)} %collective-permute-done.10, f16[288,1280]{1,0:T(8,128)(2,1)S(1)} %collective-permute-done.9, f16[288,1280]{1,0:T(8,128)(2,1)S(1)} %collective-permute-done.8, ...), kind=kOutput, calls=%fused_computation.22 | convolution fusion | flops 569180160 | bytes 7569408 | tf_op jit(solution)/shard_map/dot_general | solution.py:63
  79.9 0.9 collective-permute-start.12
  81.0 2.2 %collective-permute-start.13 = (f16[72,1280]{1,0:T(8,128)(2,1)S(1)}, f16[72,1280]{1,0:T(8,128)(2,1)S(1)}, u32[]{:S(2)}, u32[]{:S(2)}) collective-permute-start(f16[72,1280]{1,0:T(8,128)(2,1)S(1)} %get-tuple-element.32), channel_id=1, source_target_pairs={{0,3},{1,0},{2,1},{3,2},{4,7},{5,4},{6,5},{7,6},{8,11},{9,8},{10,9... | collective-permute-start | bytes 552968 | tf_op jit(solution)/shard_map/ppermute | solution.py:28
  83.4 5.5 %collective-permute-done.11 = f16[72,1280]{1,0:T(8,128)(2,1)S(1)} collective-permute-done((f16[72,1280]{1,0:T(8,128)(2,1)S(1)}, f16[72,1280]{1,0:T(8,128)(2,1)S(1)}, u32[]{:S(2)}, u32[]{:S(2)}) %collective-permute-start.11) | collective-permute-done | bytes 184352 | tf_op jit(solution)/shard_map/ppermute | solution.py:28
  88.9 2.5 %collective-permute-done.12 = f16[72,1280]{1,0:T(8,128)(2,1)S(1)} collective-permute-done((f16[72,1280]{1,0:T(8,128)(2,1)S(1)}, f16[72,1280]{1,0:T(8,128)(2,1)S(1)}, u32[]{:S(2)}, u32[]{:S(2)}) %collective-permute-start.12) | collective-permute-done | bytes 184352 | tf_op jit(solution)/shard_map/ppermute | solution.py:28
  92.2 22.6 %all_to_all.10 = f16[8,180,128]{2,1,0:T(8,128)(2,1)S(1)} all-to-all(f16[8,180,128]{2,1,0:T(8,128)(2,1)S(1)} %reshape.146), channel_id=1, replica_groups=mesh['yh'=2,'core'=2,'yl'=2,'z'=8,'x'=4] {'z'}, dimensions={0} | all-to-all | bytes 737280 | tf_op jit(solution)/shard_map/all_to_all | solution.py:168
  116.4 3.4 %all-to-all-start.1 = ((bf16[8,120,128]{2,1,0:T(8,128)(2,1)}), bf16[8,120,128]{2,1,0:T(8,128)(2,1)S(1)}, u32[]{:S(2)}, u32[]{:S(2)}) async-start(bf16[8,120,128]{2,1,0:T(8,128)(2,1)} %broadcast_in_dim.5), calls=%async_computation.1 | async-start | bytes 491520 | tf_op jit(solution)/shard_map/all_to_all | solution.py:175
  120.9 1.4 collective-permute-start.19
  122.3 1.9 %collective-permute-start.20 = (bf16[60,128]{1,0:T(8,128)(2,1)S(1)}, bf16[60,128]{1,0:T(8,128)(2,1)S(1)}, u32[]{:S(2)}, u32[]{:S(2)}) collective-permute-start(bf16[60,128]{1,0:T(8,128)(2,1)S(1)} %reshape.148), channel_id=1, source_target_pairs={{0,3},{1,0},{2,1},{3,2},{4,7},{5,4},{6,5},{7,6},{8,11},{9,8},{10,9... | collective-permute-start | bytes 46088 | tf_op jit(solution)/shard_map/ppermute | solution.py:28
  124.3 1.6 collective-permute-done.18
  126.9 1.4 collective-permute-start.21
  128.3 3.0 %collective-permute-done.21 = bf16[240,128]{1,0:T(8,128)(2,1)S(1)} collective-permute-done((bf16[240,128]{1,0:T(8,128)(2,1)S(1)}, bf16[240,128]{1,0:T(8,128)(2,1)S(1)}, u32[]{:S(2)}, u32[]{:S(2)}) %collective-permute-start.21) | collective-permute-done | bytes 61472 | tf_op jit(solution)/shard_map/ppermute | solution.py:36
  132.2 1.4 collective-permute-start.14
  133.6 4.9 %collective-permute-done.14 = bf16[48,2560]{1,0:T(8,128)(2,1)S(1)} collective-permute-done((bf16[48,2560]{1,0:T(8,128)(2,1)S(1)}, bf16[48,2560]{1,0:T(8,128)(2,1)S(1)}, u32[]{:S(2)}, u32[]{:S(2)}) %collective-permute-start.14) | collective-permute-done | bytes 245792 | tf_op jit(solution)/shard_map/ppermute | solution.py:36
  138.5 2.2 %collective-permute-start.15 = (bf16[96,2560]{1,0:T(8,128)(2,1)S(1)}, bf16[96,2560]{1,0:T(8,128)(2,1)S(1)}, u32[]{:S(2)}, u32[]{:S(2)}) collective-permute-start(bf16[96,2560]{1,0:T(8,128)(2,1)S(1)} %get-tuple-element.34), channel_id=1, source_target_pairs={{0,1},{1,2},{2,3},{3,0},{4,5},{5,6},{6,7},{7,4},{8,9},{9,10},{10,1... | collective-permute-start | bytes 1474568 | tf_op jit(solution)/shard_map/ppermute | solution.py:28
  140.6 28.3 %all_gather.3 = bf16[192,2560]{1,0:T(8,128)(2,1)S(1)} all-gather(bf16[24,2560]{1,0:T(8,128)(2,1)S(1)} %reshape.149), channel_id=1, replica_groups=mesh['yh'=2,'core'=2,'yl'=2,'z'=8,'x'=4] {'z'}, dimensions={0}, use_global_device_ids=true | all-gather | bytes 1105920 | tf_op jit(solution)/shard_map/all_gather | solution.py:182
  168.9 2.0 %collective-permute-start.16 = (bf16[96,2560]{1,0:T(8,128)(2,1)S(1)}, bf16[96,2560]{1,0:T(8,128)(2,1)S(1)}, u32[]{:S(2)}, u32[]{:S(2)}) collective-permute-start(bf16[96,2560]{1,0:T(8,128)(2,1)S(1)} %get-tuple-element.34), channel_id=1, source_target_pairs={{0,2},{1,3},{2,0},{3,1},{4,6},{5,7},{6,4},{7,5},{8,10},{9,11},{10,... | collective-permute-start | bytes 1474568 | tf_op jit(solution)/shard_map/ppermute | solution.py:28
  171.0 1.4 convolution_convert_fusion.1
  173.0 6.2 %collective-permute-done.16 = bf16[96,2560]{1,0:T(8,128)(2,1)S(1)} collective-permute-done((bf16[96,2560]{1,0:T(8,128)(2,1)S(1)}, bf16[96,2560]{1,0:T(8,128)(2,1)S(1)}, u32[]{:S(2)}, u32[]{:S(2)}) %collective-permute-start.16) | collective-permute-done | bytes 491552 | tf_op jit(solution)/shard_map/ppermute | solution.py:28
  179.3 3.9 %collective-permute-done.17 = bf16[96,2560]{1,0:T(8,128)(2,1)S(1)} collective-permute-done((bf16[96,2560]{1,0:T(8,128)(2,1)S(1)}, bf16[96,2560]{1,0:T(8,128)(2,1)S(1)}, u32[]{:S(2)}, u32[]{:S(2)}) %collective-permute-start.17) | collective-permute-done | bytes 491552 | tf_op jit(solution)/shard_map/ppermute | solution.py:28
  183.2 2.5 %convolution_convert_fusion = bf16[384,2560]{1,0:T(8,128)(2,1)} fusion(bf16[384,2560]{1,0:T(8,128)(2,1)S(1)} %constant_dynamic-update-slice_fusion.2, s32[384]{0:T(512)S(1)} %fusion.77), kind=kOutput, calls=%fused_computation | convolution fusion | flops 756105216 | bytes 3933696 | tf_op jit(solution)/shard_map/dot_general | solution.py:63
  (82 shorter events, 13.9 us)
Async XLA Ops:
  2.1 1.7 copy-start
  3.7 1.2 copy-start.2
  4.9 1.0 copy-start.4
  5.9 0.9 copy-start.6
  6.8 4.1 %copy-start.1 = (bf16[768,1536]{1,0:T(8,128)(2,1)S(1)}, bf16[768,1536]{1,0:T(8,128)(2,1)}, u32[]{:S(2)}) copy-start(bf16[768,1536]{1,0:T(8,128)(2,1)} %shared_ref.3) | copy-start | bytes 7077892
  6.8 4.1 %copy-start.3 = (bf16[2,576,384]{2,1,0:T(8,128)(2,1)S(1)}, bf16[2,576,384]{2,1,0:T(8,128)(2,1)}, u32[]{:S(2)}) copy-start(bf16[2,576,384]{2,1,0:T(8,128)(2,1)} %constant.260.clone.routed_order_ref) | copy-start | bytes 2654212
  6.8 4.1 %copy-start.7 = (bf16[96,768]{1,0:T(8,128)(2,1)S(1)}, bf16[96,768]{1,0:T(8,128)(2,1)}, u32[]{:S(2)}) copy-start(bf16[96,768]{1,0:T(8,128)(2,1)} %routed_ref.3) | copy-start | bytes 442372
  10.4 4.3 %collective-permute-start = (bf16[4,2,144,768]{3,2,1,0:T(8,128)(2,1)}, bf16[4,2,144,768]{3,2,1,0:T(8,128)(2,1)}, u32[]{:S(2)}, u32[]{:S(2)}) collective-permute-start(bf16[4,2,144,768]{3,2,1,0:T(8,128)(2,1)} %shard_map.173), channel_id=1, source_target_pairs={{0,64},{64,0},{1,65},{65,1},{2,66},{66,2},{3,67},{67,3},{4,68},{68... | collective-permute-start | bytes 5308424 | tf_op jit(solution)/shard_map/ppermute | solution.py:40
  10.4 13.8 %collective-permute-start.1 = (bf16[768,2560]{1,0:T(8,128)(2,1)}, bf16[768,2560]{1,0:T(8,128)(2,1)}, u32[]{:S(2)}, u32[]{:S(2)}) collective-permute-start(bf16[768,2560]{1,0:T(8,128)(2,1)} %param.15), channel_id=1, source_target_pairs={{0,64},{64,0},{1,65},{65,1},{2,66},{66,2},{3,67},{67,3},{4,68},{68... | collective-permute-start | bytes 11796488 | tf_op jit(solution)/shard_map/ppermute | solution.py:40
  10.9 1.0 copy-start.5
  16.3 2.6 %copy-start.14 = (bf16[768,2560]{1,0:T(8,128)(2,1)S(1)}, bf16[768,2560]{1,0:T(8,128)(2,1)}, u32[]{:S(2)}) copy-start(bf16[768,2560]{1,0:T(8,128)(2,1)} %param.15) | copy-start | bytes 11796484
  26.6 21.0 %collective-permute-start.2 = (f16[288,1280]{1,0:T(8,128)(2,1)S(1)}, f16[288,1280]{1,0:T(8,128)(2,1)S(1)}, u32[]{:S(2)}, u32[]{:S(2)}) collective-permute-start(f16[288,1280]{1,0:T(8,128)(2,1)S(1)} %fusion.19), channel_id=1, source_target_pairs={{0,2},{1,3},{2,0},{3,1},{4,6},{5,7},{6,4},{7,5},{8,10},{9,11},{10,... | collective-permute-start | bytes 2211848 | tf_op jit(solution)/shard_map/ppermute | solution.py:28
  32.0 30.4 %collective-permute-start.3 = (f16[288,1280]{1,0:T(8,128)(2,1)S(1)}, f16[288,1280]{1,0:T(8,128)(2,1)S(1)}, u32[]{:S(2)}, u32[]{:S(2)}) collective-permute-start(f16[288,1280]{1,0:T(8,128)(2,1)S(1)} %fusion.18), channel_id=1, source_target_pairs={{0,1},{1,2},{2,3},{3,0},{4,5},{5,6},{6,7},{7,4},{8,9},{9,10},{10,1... | collective-permute-start | bytes 2211848 | tf_op jit(solution)/shard_map/ppermute | solution.py:28
  35.0 27.5 %collective-permute-start.4 = (f16[288,1280]{1,0:T(8,128)(2,1)S(1)}, f16[288,1280]{1,0:T(8,128)(2,1)S(1)}, u32[]{:S(2)}, u32[]{:S(2)}) collective-permute-start(f16[288,1280]{1,0:T(8,128)(2,1)S(1)} %fusion.17), channel_id=1, source_target_pairs={{0,3},{1,0},{2,1},{3,2},{4,7},{5,4},{6,5},{7,6},{8,11},{9,8},{10,9... | collective-permute-start | bytes 2211848 | tf_op jit(solution)/shard_map/ppermute | solution.py:28
  40.2 27.5 %collective-permute-start.8 = (f16[288,1280]{1,0:T(8,128)(2,1)S(1)}, f16[288,1280]{1,0:T(8,128)(2,1)S(1)}, u32[]{:S(2)}, u32[]{:S(2)}) collective-permute-start(f16[288,1280]{1,0:T(8,128)(2,1)S(1)} %fusion.16), channel_id=1, source_target_pairs={{0,128},{32,160},{128,0},{160,32},{1,129},{33,161},{129,1},{161,33... | collective-permute-start | bytes 2211848 | tf_op jit(solution)/shard_map/ppermute | solution.py:32
  43.0 34.2 %collective-permute-start.9 = (f16[288,1280]{1,0:T(8,128)(2,1)S(1)}, f16[288,1280]{1,0:T(8,128)(2,1)S(1)}, u32[]{:S(2)}, u32[]{:S(2)}) collective-permute-start(f16[288,1280]{1,0:T(8,128)(2,1)S(1)} %fusion.15), channel_id=1, source_target_pairs={{0,32},{32,128},{128,160},{160,0},{1,33},{33,129},{129,161},{161,1... | collective-permute-start | bytes 2211848 | tf_op jit(solution)/shard_map/ppermute | solution.py:32
  47.6 29.6 %collective-permute-start.10 = (f16[288,1280]{1,0:T(8,128)(2,1)S(1)}, f16[288,1280]{1,0:T(8,128)(2,1)S(1)}, u32[]{:S(2)}, u32[]{:S(2)}) collective-permute-start(f16[288,1280]{1,0:T(8,128)(2,1)S(1)} %fusion.14), channel_id=1, source_target_pairs={{0,160},{32,0},{128,32},{160,128},{1,161},{33,1},{129,33},{161,129... | collective-permute-start | bytes 2211848 | tf_op jit(solution)/shard_map/ppermute | solution.py:32
  65.1 15.9 %collective-permute-start.5 = (f16[72,1280]{1,0:T(8,128)(2,1)S(1)}, f16[72,1280]{1,0:T(8,128)(2,1)S(1)}, u32[]{:S(2)}, u32[]{:S(2)}) collective-permute-start(f16[72,1280]{1,0:T(8,128)(2,1)S(1)} %get-tuple-element.28), channel_id=1, source_target_pairs={{0,128},{32,160},{128,0},{160,32},{1,129},{33,161},{129,1},{161,33... | collective-permute-start | bytes 552968 | tf_op jit(solution)/shard_map/ppermute | solution.py:32
  67.2 16.0 %collective-permute-start.6 = (f16[72,1280]{1,0:T(8,128)(2,1)S(1)}, f16[72,1280]{1,0:T(8,128)(2,1)S(1)}, u32[]{:S(2)}, u32[]{:S(2)}) collective-permute-start(f16[72,1280]{1,0:T(8,128)(2,1)S(1)} %get-tuple-element.30), channel_id=1, source_target_pairs={{0,32},{32,128},{128,160},{160,0},{1,33},{33,129},{129,161},{161,1... | collective-permute-start | bytes 552968 | tf_op jit(solution)/shard_map/ppermute | solution.py:32
  67.8 15.5 %collective-permute-start.7 = (f16[72,1280]{1,0:T(8,128)(2,1)S(1)}, f16[72,1280]{1,0:T(8,128)(2,1)S(1)}, u32[]{:S(2)}, u32[]{:S(2)}) collective-permute-start(f16[72,1280]{1,0:T(8,128)(2,1)S(1)} %get-tuple-element.29), channel_id=1, source_target_pairs={{0,160},{32,0},{128,32},{160,128},{1,161},{33,1},{129,33},{161,129... | collective-permute-start | bytes 552968 | tf_op jit(solution)/shard_map/ppermute | solution.py:32
  79.8 9.1 %collective-permute-start.11 = (f16[72,1280]{1,0:T(8,128)(2,1)S(1)}, f16[72,1280]{1,0:T(8,128)(2,1)S(1)}, u32[]{:S(2)}, u32[]{:S(2)}) collective-permute-start(f16[72,1280]{1,0:T(8,128)(2,1)S(1)} %get-tuple-element.31), channel_id=1, source_target_pairs={{0,2},{1,3},{2,0},{3,1},{4,6},{5,7},{6,4},{7,5},{8,10},{9,11},{10,... | collective-permute-start | bytes 552968 | tf_op jit(solution)/shard_map/ppermute | solution.py:28
  79.9 11.6 %collective-permute-start.12 = (f16[72,1280]{1,0:T(8,128)(2,1)S(1)}, f16[72,1280]{1,0:T(8,128)(2,1)S(1)}, u32[]{:S(2)}, u32[]{:S(2)}) collective-permute-start(f16[72,1280]{1,0:T(8,128)(2,1)S(1)} %get-tuple-element.33), channel_id=1, source_target_pairs={{0,1},{1,2},{2,3},{3,0},{4,5},{5,6},{6,7},{7,4},{8,9},{9,10},{10,1... | collective-permute-start | bytes 552968 | tf_op jit(solution)/shard_map/ppermute | solution.py:28
  81.0 10.4 %collective-permute-start.13 = (f16[72,1280]{1,0:T(8,128)(2,1)S(1)}, f16[72,1280]{1,0:T(8,128)(2,1)S(1)}, u32[]{:S(2)}, u32[]{:S(2)}) collective-permute-start(f16[72,1280]{1,0:T(8,128)(2,1)S(1)} %get-tuple-element.32), channel_id=1, source_target_pairs={{0,3},{1,0},{2,1},{3,2},{4,7},{5,4},{6,5},{7,6},{8,11},{9,8},{10,9... | collective-permute-start | bytes 552968 | tf_op jit(solution)/shard_map/ppermute | solution.py:28
  83.4 31.5 %copy-start.8 = (f32[6,2560]{1,0:T(8,128)S(1)}, f32[6,2560]{1,0:T(8,128)}, u32[]{:S(2)}) copy-start(f32[6,2560]{1,0:T(8,128)} %param.18) | copy-start | bytes 184324
  83.4 31.5 %copy-start.9 = (f32[6,2560]{1,0:T(8,128)S(1)}, f32[6,2560]{1,0:T(8,128)}, u32[]{:S(2)}) copy-start(f32[6,2560]{1,0:T(8,128)} %param.20) | copy-start | bytes 184324
  83.4 31.5 %copy-start.10 = (f32[6,2560]{1,0:T(8,128)S(1)}, f32[6,2560]{1,0:T(8,128)}, u32[]{:S(2)}) copy-start(f32[6,2560]{1,0:T(8,128)} %param.19) | copy-start | bytes 184324
  91.7 28.2 %copy-start.11 = (f32[3,2560]{1,0:T(4,128)S(1)}, f32[3,2560]{1,0:T(4,128)}, u32[]{:S(2)}) copy-start(f32[3,2560]{1,0:T(4,128)} %param.21) | copy-start | bytes 92164
  91.7 28.2 %copy-start.12 = (f32[3,2560]{1,0:T(4,128)S(1)}, f32[3,2560]{1,0:T(4,128)}, u32[]{:S(2)}) copy-start(f32[3,2560]{1,0:T(4,128)} %param.23) | copy-start | bytes 92164
  91.7 28.2 %copy-start.13 = (f32[3,2560]{1,0:T(4,128)S(1)}, f32[3,2560]{1,0:T(4,128)}, u32[]{:S(2)}) copy-start(f32[3,2560]{1,0:T(4,128)} %param.22) | copy-start | bytes 92164
  116.4 15.4 %all-to-all-start.1 = ((bf16[8,120,128]{2,1,0:T(8,128)(2,1)}), bf16[8,120,128]{2,1,0:T(8,128)(2,1)S(1)}, u32[]{:S(2)}, u32[]{:S(2)}) async-start(bf16[8,120,128]{2,1,0:T(8,128)(2,1)} %broadcast_in_dim.5), calls=%async_computation.1 | async-start | bytes 491520 | tf_op jit(solution)/shard_map/all_to_all | solution.py:175
  120.6 5.2 %collective-permute-start.18 = (bf16[60,128]{1,0:T(8,128)(2,1)S(1)}, bf16[60,128]{1,0:T(8,128)(2,1)S(1)}, u32[]{:S(2)}, u32[]{:S(2)}) collective-permute-start(bf16[60,128]{1,0:T(8,128)(2,1)S(1)} %reshape.148), channel_id=1, source_target_pairs={{0,1},{1,2},{2,3},{3,0},{4,5},{5,6},{6,7},{7,4},{8,9},{9,10},{10,1... | collective-permute-start | bytes 46088 | tf_op jit(solution)/shard_map/ppermute | solution.py:28
  120.9 5.3 %collective-permute-start.19 = (bf16[60,128]{1,0:T(8,128)(2,1)S(1)}, bf16[60,128]{1,0:T(8,128)(2,1)S(1)}, u32[]{:S(2)}, u32[]{:S(2)}) collective-permute-start(bf16[60,128]{1,0:T(8,128)(2,1)S(1)} %reshape.148), channel_id=1, source_target_pairs={{0,2},{1,3},{2,0},{3,1},{4,6},{5,7},{6,4},{7,5},{8,10},{9,11},{10,... | collective-permute-start | bytes 46088 | tf_op jit(solution)/shard_map/ppermute | solution.py:28
  122.3 4.6 %collective-permute-start.20 = (bf16[60,128]{1,0:T(8,128)(2,1)S(1)}, bf16[60,128]{1,0:T(8,128)(2,1)S(1)}, u32[]{:S(2)}, u32[]{:S(2)}) collective-permute-start(bf16[60,128]{1,0:T(8,128)(2,1)S(1)} %reshape.148), channel_id=1, source_target_pairs={{0,3},{1,0},{2,1},{3,2},{4,7},{5,4},{6,5},{7,6},{8,11},{9,8},{10,9... | collective-permute-start | bytes 46088 | tf_op jit(solution)/shard_map/ppermute | solution.py:28
  126.9 4.4 %collective-permute-start.21 = (bf16[240,128]{1,0:T(8,128)(2,1)S(1)}, bf16[240,128]{1,0:T(8,128)(2,1)S(1)}, u32[]{:S(2)}, u32[]{:S(2)}) collective-permute-start(bf16[240,128]{1,0:T(8,128)(2,1)S(1)} %pad_maximum_fusion.1), channel_id=1, source_target_pairs={{0,32},{32,0},{1,33},{33,1},{2,34},{34,2},{3,35},{35,3},{4,36},{36... | collective-permute-start | bytes 184328 | tf_op jit(solution)/shard_map/ppermute | solution.py:36
  132.2 6.3 %collective-permute-start.14 = (bf16[48,2560]{1,0:T(8,128)(2,1)S(1)}, bf16[48,2560]{1,0:T(8,128)(2,1)S(1)}, u32[]{:S(2)}, u32[]{:S(2)}) collective-permute-start(bf16[48,2560]{1,0:T(8,128)(2,1)S(1)} %reshape.147), channel_id=1, source_target_pairs={{0,32},{32,0},{1,33},{33,1},{2,34},{34,2},{3,35},{35,3},{4,36},{36... | collective-permute-start | bytes 737288 | tf_op jit(solution)/shard_map/ppermute | solution.py:36
  138.5 34.5 %collective-permute-start.15 = (bf16[96,2560]{1,0:T(8,128)(2,1)S(1)}, bf16[96,2560]{1,0:T(8,128)(2,1)S(1)}, u32[]{:S(2)}, u32[]{:S(2)}) collective-permute-start(bf16[96,2560]{1,0:T(8,128)(2,1)S(1)} %get-tuple-element.34), channel_id=1, source_target_pairs={{0,1},{1,2},{2,3},{3,0},{4,5},{5,6},{6,7},{7,4},{8,9},{9,10},{10,1... | collective-permute-start | bytes 1474568 | tf_op jit(solution)/shard_map/ppermute | solution.py:28
  168.9 10.3 %collective-permute-start.16 = (bf16[96,2560]{1,0:T(8,128)(2,1)S(1)}, bf16[96,2560]{1,0:T(8,128)(2,1)S(1)}, u32[]{:S(2)}, u32[]{:S(2)}) collective-permute-start(bf16[96,2560]{1,0:T(8,128)(2,1)S(1)} %get-tuple-element.34), channel_id=1, source_target_pairs={{0,2},{1,3},{2,0},{3,1},{4,6},{5,7},{6,4},{7,5},{8,10},{9,11},{10,... | collective-permute-start | bytes 1474568 | tf_op jit(solution)/shard_map/ppermute | solution.py:28
  172.4 10.8 %collective-permute-start.17 = (bf16[96,2560]{1,0:T(8,128)(2,1)S(1)}, bf16[96,2560]{1,0:T(8,128)(2,1)S(1)}, u32[]{:S(2)}, u32[]{:S(2)}) collective-permute-start(bf16[96,2560]{1,0:T(8,128)(2,1)S(1)} %get-tuple-element.34), channel_id=1, source_target_pairs={{0,3},{1,0},{2,1},{3,2},{4,7},{5,4},{6,5},{7,6},{8,11},{9,8},{10,9... | collective-permute-start | bytes 1474568 | tf_op jit(solution)/shard_map/ppermute | solution.py:28
